TPU v7x, 512 devices: a whole 4x8x8 slice. The times are simulated.
512 devices in a mesh: ja: 128 (over z, y, core), ia: 4 (over x).
Axes of the slice: x: 4, y: 8, z: 8, core: 2. Of those that a mesh axis runs over, the one named last changes fastest.
Arguments:
- positions: float32 [3, 131072], P(None, 'ja'), may hold values from -1 to 1
- velocities: float32 [3, 131072], P(None, 'ja'), may hold values from -3 to 3
- accels: float32 [3, 131072], P(None, 'ja'), may hold values from -3 to 3
- jerks: float32 [3, 131072], P(None, 'ja'), may hold values from -6 to 6
- masses: float32 [131072], P('ja'), may hold values from 2.2888185e-06 to 2.2888184e-05
- last_time: float32 [131072], P('ja'), may hold values from -0.25 to 0
- active: int32 [2, 4096], replicated, may hold values from 0 to 131071, as said below
Outputs:
- new_positions: float32 [3, 131072], P(None, 'ja')
- new_velocities: float32 [3, 131072], P(None, 'ja')
- new_accels: float32 [3, 131072], P(None, 'ja')
- new_jerks: float32 [3, 131072], P(None, 'ja')
- new_times: float32 [131072], P('ja')
- active_state: float32 [2, 12, 4096], replicated
Inputs may be any that keep to these rules, and one draw needn't show every extreme that they name: `active`: each row lists 4096 distinct star indices and names both star 0 and star 131072 - 1.
All inputs are finite; a program needn't handle non-finite values.
Results may differ from a plain program's by a relative error of at most 0.0001.
Values sent between devices are 32-bit elements; how exact they have to be, the bound alone decides.
A program may use at most 64 MiB of HBM per device.

v0:
```python
import math

import jax
import jax.numpy as jnp
from jax import lax
from jax.sharding import PartitionSpec as P

step_length = 0.0625
soft_sq = 0.0025


def predict(positions, velocities, accels, jerks, elapsed):
    pred_pos = positions + elapsed * (velocities + elapsed * (accels / 2.0 + elapsed * jerks / 6.0))
    pred_vel = velocities + elapsed * (accels + elapsed * jerks / 2.0)
    return (pred_pos, pred_vel)


def pair_sums(act_pos, act_vel, field_pos, field_vel, field_mass):
    sep_pos = field_pos[:, None, :] - act_pos[:, :, None]
    sep_vel = field_vel[:, None, :] - act_vel[:, :, None]
    dist_sq = soft_sq + jnp.sum(sep_pos * sep_pos, axis=0)
    inv_dist = 1.0 / jnp.sqrt(dist_sq)
    weight = field_mass[None, :] * inv_dist * inv_dist * inv_dist
    radial = 3.0 * jnp.sum(sep_pos * sep_vel, axis=0) / dist_sq
    acc_sum = jnp.sum(sep_pos * weight[None], axis=-1)
    jerk_sum = jnp.sum((sep_vel - radial[None] * sep_pos) * weight[None], axis=-1)
    return (acc_sum, jerk_sum)


def block_forces(act_pos, act_vel, field_pos, field_vel, field_mass):
    act_block = math.gcd(act_pos.shape[1], 512)
    field_block = math.gcd(field_pos.shape[1], 512)
    act_count = act_pos.shape[1] // act_block
    field_count = field_pos.shape[1] // field_block
    act_blocks = (
        act_pos.reshape(3, act_count, act_block).transpose(1, 0, 2),
        act_vel.reshape(3, act_count, act_block).transpose(1, 0, 2),
    )
    field_blocks = (
        field_pos.reshape(3, field_count, field_block).transpose(1, 0, 2),
        field_vel.reshape(3, field_count, field_block).transpose(1, 0, 2),
        field_mass.reshape(field_count, field_block),
    )

    def one_block(pieces):
        block_pos, block_vel = pieces

        def visit(carry, field_piece):
            acc_sum, jerk_sum = pair_sums(
                block_pos, block_vel, field_piece[0], field_piece[1], field_piece[2]
            )
            return ((carry[0] + acc_sum, carry[1] + jerk_sum), None)

        start = (jnp.zeros_like(block_pos), jnp.zeros_like(block_pos))
        totals, unused = lax.scan(visit, start, field_blocks)
        return jnp.concatenate([totals[0], totals[1]], axis=0)

    result = lax.map(one_block, act_blocks)
    return result.transpose(1, 0, 2).reshape(6, -1)


def correct(packet, forces):
    pred_pos = packet[0:3]
    pred_vel = packet[3:6]
    old_acc = packet[6:9]
    old_jerk = packet[9:12]
    elapsed = packet[12:13]
    new_acc = forces[0:3]
    new_jerk = forces[3:6]
    elapsed_sq = elapsed * elapsed
    acc_diff = old_acc - new_acc
    snap_coef = (-6.0 * acc_diff - elapsed * (4.0 * old_jerk + 2.0 * new_jerk)) / elapsed_sq
    crackle = (12.0 * acc_diff + 6.0 * elapsed * (old_jerk + new_jerk)) / (elapsed_sq * elapsed)
    new_pos = (
        pred_pos
        + elapsed_sq * elapsed_sq / 24.0 * snap_coef
        + elapsed_sq * elapsed_sq * elapsed / 120.0 * crackle
    )
    new_vel = (
        pred_vel + elapsed_sq * elapsed / 6.0 * snap_coef + elapsed_sq * elapsed_sq / 24.0 * crackle
    )
    return jnp.concatenate([new_pos, new_vel, new_acc, new_jerk], axis=0)


def per_device(positions, velocities, accels, jerks, masses, last_time, active):
    field_count = positions.shape[1]
    ia_count = lax.axis_size("ia")
    ja_count = lax.axis_size("ja")
    act_dev = active.shape[1] // ia_count
    share_count = act_dev // ja_count
    my_ia = lax.axis_index("ia")
    my_ja = lax.axis_index("ja")
    states = []
    for section_num in range(2):
        time_now = step_length * (section_num + 1)
        elapsed = time_now - last_time
        pred_pos, pred_vel = predict(positions, velocities, accels, jerks, elapsed)
        packet = jnp.concatenate([pred_pos, pred_vel, accels, jerks, elapsed[None]], axis=0)
        chosen = lax.dynamic_slice_in_dim(active[section_num], my_ia * act_dev, act_dev)
        local_idx = chosen - my_ja * field_count
        is_owned = (local_idx >= 0) & (local_idx < field_count)
        safe_idx = jnp.where(is_owned, local_idx, 0)
        picked = jnp.where(is_owned[None, :], jnp.take(packet, safe_idx, axis=1), 0.0)
        act_rows = lax.psum(picked, "ja")
        partial_value = block_forces(act_rows[0:3], act_rows[3:6], pred_pos, pred_vel, masses)
        summed = lax.psum_scatter(partial_value, "ja", scatter_dimension=1, tiled=True)
        share_rows = lax.dynamic_slice_in_dim(act_rows, my_ja * share_count, share_count, 1)
        fresh_rows = correct(share_rows, summed)
        gathered = lax.all_gather(fresh_rows, ("ja", "ia"), axis=1, tiled=True)
        corrected = (
            gathered.reshape(12, ja_count, ia_count, share_count)
            .transpose(0, 2, 1, 3)
            .reshape(12, -1)
        )
        states.append(corrected)
        row_order = active[section_num]
        target = row_order - my_ja * field_count
        target = jnp.where((target >= 0) & (target < field_count), target, field_count)
        positions = positions.at[:, target].set(corrected[0:3], mode="drop")
        velocities = velocities.at[:, target].set(corrected[3:6], mode="drop")
        accels = accels.at[:, target].set(corrected[6:9], mode="drop")
        jerks = jerks.at[:, target].set(corrected[9:12], mode="drop")
        last_time = last_time.at[target].set(jnp.zeros_like(corrected[0]) + time_now, mode="drop")
    return (positions, velocities, accels, jerks, last_time, jnp.stack(states))


def solution(mesh):
    in_specs = (P(None, "ja"), P(None, "ja"), P(None, "ja"), P(None, "ja"), P("ja"), P("ja"), P())
    out_specs = (P(None, "ja"), P(None, "ja"), P(None, "ja"), P(None, "ja"), P("ja"), P())
    return jax.shard_map(
        per_device, mesh=mesh, in_specs=in_specs, out_specs=out_specs, check_vma=False
    )
```

profile of v0, /device:TPU:1, one launch (start us, length us, event | category | flops | bytes accessed | tf_op | source)
XLA Modules:
  0.0 2409.0 jit_solution(14779390855428095170)
XLA Ops:
  6.6 15.5 scatter_fusion.1
  22.2 15.5 scatter_fusion.9
  41.3 498.1 %psum.14 = f32[13,1024]{0,1:T(8,128)S(1)} all-reduce(f32[13,1024]{0,1:T(8,128)S(1)} %bitcast_select_fusion.1), channel_id=1, replica_groups=mesh['ja'=128,'ia'=4] {'ja'}, use_global_device_ids=true, to_apply=%region_0.2 | all-reduce | flops 13312 | bytes 106496 | tf_op jit(solution)/shard_map/psum | solution.py:104
  544.5 11.3 while.47
  544.5 5.6 while.50
  550.2 5.6 while.50
  556.0 490.9 %all-reduce = f32[6,1024]{0,1:T(8,128)S(1)} all-reduce(f32[6,1024]{0,1:T(8,128)S(1)} %bitcast.139), channel_id=2, replica_groups=mesh['ja'=128,'ia'=4] {'ja'}, use_global_device_ids=true, to_apply=%region_9.11.clone | all-reduce | flops 6144 | bytes 49152
  1047.2 113.8 %all_gather.6 = f32[12,4096]{0,1:T(8,128)} all-gather(f32[12,8]{0,1:T(8,128)S(1)} %pad_maximum_fusion.1), channel_id=1, replica_groups=mesh['ja'=128,'ia'=4] {'ja','ia'}, dimensions={1}, use_global_device_ids=true | all-gather | bytes 196992 | tf_op jit(solution)/shard_map/all_gather | solution.py:109
  1161.0 5.3 copy.240
  1178.3 11.1 scatter_fusion
  1191.6 11.1 scatter_fusion.2
  1205.0 11.7 scatter_fusion.3
  1218.9 11.1 scatter_fusion.4
  1233.8 489.1 %psum.15 = f32[13,1024]{0,1:T(8,128)S(1)} all-reduce(f32[13,1024]{0,1:T(8,128)S(1)} %bitcast_select_fusion), channel_id=1, replica_groups=mesh['ja'=128,'ia'=4] {'ja'}, use_global_device_ids=true, to_apply=%region_15.17 | all-reduce | flops 13312 | bytes 106496 | tf_op jit(solution)/shard_map/psum | solution.py:104
  1723.8 11.3 while.49
  1723.8 5.6 while.51
  1729.5 5.6 while.51
  1735.4 490.9 %all-reduce.1 = f32[6,1024]{0,1:T(8,128)S(1)} all-reduce(f32[6,1024]{0,1:T(8,128)S(1)} %bitcast.140), channel_id=3, replica_groups=mesh['ja'=128,'ia'=4] {'ja'}, use_global_device_ids=true, to_apply=%region_24.26.clone | all-reduce | flops 6144 | bytes 49152
  2226.5 111.5 %all_gather.7 = f32[12,4096]{0,1:T(8,128)} all-gather(f32[12,8]{0,1:T(8,128)S(1)} %pad_maximum_fusion.2), channel_id=1, replica_groups=mesh['ja'=128,'ia'=4] {'ja','ia'}, dimensions={1}, use_global_device_ids=true | all-gather | bytes 196992 | tf_op jit(solution)/shard_map/all_gather | solution.py:109
  2338.0 5.3 copy.263
  2358.0 11.1 scatter_fusion.5
  2372.0 11.1 scatter_fusion.6
  2384.6 11.0 scatter_fusion.7
  2397.1 10.8 scatter_fusion.8
  (186 shorter events, 81.2 us)
Async XLA Ops:
  22.2 15.6 copy-start.13
  22.2 15.6 copy-start.14
  37.7 506.4 %copy-start = (f32[1024]{0:T(1024)}, f32[1024]{0:T(1024)S(1)}, u32[]{:S(2)}) copy-start(f32[1024]{0:T(1024)S(1)} %scatter_fusion.9) | copy-start | bytes 12292
  37.7 502.0 %copy-start.15 = (f32[3,1024]{1,0:T(4,128)S(1)}, f32[3,1024]{1,0:T(4,128)}, u32[]{:S(2)}) copy-start(f32[3,1024]{1,0:T(4,128)} %param.17) | copy-start | bytes 36868
  37.7 503.0 %copy-start.16 = (f32[3,1024]{1,0:T(4,128)S(1)}, f32[3,1024]{1,0:T(4,128)}, u32[]{:S(2)}) copy-start(f32[3,1024]{1,0:T(4,128)} %param.18) | copy-start | bytes 36868
  1170.0 8.3 copy-start.10
  1176.3 15.4 copy-start.7
  1189.4 2.2 copy-start.11
  1189.4 15.6 copy-start.4
  1202.8 16.1 copy-start.8
  1202.8 16.1 copy-start.1
  1216.7 17.1 copy-start.5
  1230.0 493.6 %copy-start.2 = (f32[3,1024]{0,1:T(8,128)}, f32[3,1024]{0,1:T(8,128)S(1)}, u32[]{:S(2)}) copy-start(f32[3,1024]{0,1:T(8,128)S(1)} %scatter_fusion.4) | copy-start | bytes 36868
  2349.7 8.3 copy-start.12
  2356.0 16.0 copy-start.9
  2369.2 15.4 copy-start.6
  2383.1 14.0 copy-start.3
where the time goes:
time: 2410 us
  blocking collectives  2190 us (91%)
  local copies, waits for them, and re-layouts  186 us (8%)
  other arithmetic  26.2 us (1%)
    psum x2, blocking collectives, per_device(): act_rows = lax.psum(picked, 'ja')  987 us
    unnamed x2, blocking collectives  982 us
    all_gather x2, blocking collectives, per_device(): gathered = lax.all_gather(fresh_rows, ('ja', 'ia'), axis=1, tiled=True)  225 us

commit v1 on v0

v1 whole, which is shorter than its diff:
```python
import functools

import jax
import jax.numpy as jnp
from jax import lax
from jax.experimental import pallas as pl
from jax.experimental.pallas import tpu as pltpu
from jax.sharding import PartitionSpec as P

MESH = pl.DeviceIdType.MESH
F32 = jnp.float32
BF16 = jnp.bfloat16
STEP = 0.0625
SOFT_SQ = 0.0025
LANES = 128
HALF = 64
CORES = 2
RINGS = {"z": 8, "y": 8, "x": 4}


def split3(value):
    first = value.astype(BF16)
    rest = value - first.astype(F32)
    second = rest.astype(BF16)
    third = (rest - second.astype(F32)).astype(BF16)
    return first, second, third


def dot_nn(left, right):
    return lax.dot_general(left, right, (((1,), (0,)), ((), ())), preferred_element_type=F32)


def dot_nt(left, right):
    return lax.dot_general(left, right, (((1,), (1,)), ((), ())), preferred_element_type=F32)


def exact_nn(left, onehot):
    one, two, three = split3(left)
    return (dot_nn(three, onehot) + dot_nn(two, onehot)) + dot_nn(one, onehot)


def exact_nt(left, onehot):
    one, two, three = split3(left)
    return (dot_nt(three, onehot) + dot_nt(two, onehot)) + dot_nt(one, onehot)


def predict(pos, vel, acc, jerk, elapsed):
    pred_pos = pos + elapsed * (vel + elapsed * (acc / 2.0 + elapsed * jerk / 6.0))
    pred_vel = vel + elapsed * (acc + elapsed * jerk / 2.0)
    return pred_pos, pred_vel


def low_lanes():
    return lax.broadcasted_iota(jnp.int32, (8, LANES), 1) < HALF


def swap(tile):
    return pltpu.roll(tile, HALF, 1)


def pack(low, high):
    return jnp.where(low_lanes(), low, swap(high))


def pair_terms(act, field, sums):
    ax, ay, az, au, av, aw = act
    fx, fy, fz, fu, fv, fw, mass = field
    dx, dy, dz = fx - ax, fy - ay, fz - az
    du, dv, dw = fu - au, fv - av, fw - aw
    dist_sq = (dx * dx + dy * dy) + (dz * dz + SOFT_SQ)
    inv = lax.rsqrt(dist_sq)
    inv_sq = inv * inv
    weight = (mass * inv) * inv_sq
    radial = ((dx * du + dy * dv) + dz * dw) * (3.0 * inv_sq)
    return (
        sums[0] + weight * dx,
        sums[1] + weight * dy,
        sums[2] + weight * dz,
        sums[3] + weight * (du - radial * dx),
        sums[4] + weight * (dv - radial * dy),
        sums[5] + weight * (dw - radial * dz),
    )


def hops(delta, size):
    return min(delta, size - delta)


def kernel(
    sizes,
    pos_in, vel_in, acc_in, jerk_in, mass_in, last_in, act_in,
    pos_out, vel_out, acc_out, jerk_out, time_out, state_out,
    pos_v, vel_v, acc_v, jerk_v, mass_v, last_v, act_v,
    raw, src0, rs_src, rs_dst, pick_src, pick_dst, sum_src, sum_dst,
    field, gath, act_cols, sums_v, corr, low_hot, match, column, scat, fresh,
    in_sem, rs_s, rs_r, pick_s, pick_r, sum_s, sum_r, fz_s, fz_r, fc_s, fc_r,
    ag_s, ag_r, agc_s, agc_r,
):
    zs, ys, xs = sizes
    total = xs * zs * LANES
    quarter = zs * LANES
    ja = lax.axis_index("ja")
    x = lax.axis_index("ia")
    z = lax.div(ja, ys * CORES)
    y = lax.rem(lax.div(ja, CORES), ys)
    c = lax.rem(ja, CORES)

    def device(dz, dy, dc, dx):
        pz = lax.rem(z + dz, zs)
        py = lax.rem(y + dy, ys)
        pc = lax.rem(c + dc, CORES)
        return ((pz * ys + py) * CORES + pc, lax.rem(x + dx, xs))

    zc_list = sorted(
        [(dz, dc) for dz in range(zs) for dc in range(CORES) if (dz, dc) != (0, 0)],
        key=lambda p: -hops(p[0], zs),
    )
    xz_list = sorted(
        [(dz, dx) for dz in range(zs) for dx in range(xs) if (dz, dx) != (0, 0)],
        key=lambda p: -hops(p[0], zs) - hops(p[1], xs),
    )
    y_list = sorted(range(1, ys), key=lambda p: -hops(p, ys))
    z_list = sorted(range(1, zs), key=lambda p: hops(p, zs))
    started = []

    def send(src, dst, ssem, rsem, target):
        copy = pltpu.make_async_remote_copy(
            src_ref=src, dst_ref=dst, send_sem=ssem, recv_sem=rsem,
            device_id=target, device_id_type=MESH,
        )
        copy.start()
        started.append(copy)
        return copy

    loads = [
        pltpu.make_async_copy(a, b, in_sem.at[n])
        for n, (a, b) in enumerate(
            [(pos_in, pos_v), (vel_in, vel_v), (acc_in, acc_v), (jerk_in, jerk_v),
             (mass_in, mass_v), (last_in, last_v), (act_in, act_v)]
        )
    ]
    for load in loads:
        load.start()
    barrier = pltpu.get_barrier_semaphore()
    partners = [(dz, 0, dc, 0) for dz, dc in zc_list]
    partners += [(0, dy, 0, 0) for dy in y_list]
    partners += [(dz, 0, 0, dx) for dz, dx in xz_list if dx != 0]
    for partner in partners:
        pl.semaphore_signal(barrier, inc=1, device_id=device(*partner), device_id_type=MESH)
    for load in loads:
        load.wait()

    for ref, at in ((pos_v, 0), (vel_v, 3), (acc_v, 8), (jerk_v, 11)):
        for comp in range(3):
            for hi in range(8):
                row = (at + comp) * 8 + hi
                raw[row : row + 1, :] = ref[comp : comp + 1, hi * LANES : (hi + 1) * LANES]
    raw[48:56, :] = last_v[...]
    raw[56:64, :] = mass_v[...]

    def value(ref, n):
        return ref[n * 8 : n * 8 + 8, :]

    def predicted(time_now):
        elapsed = time_now - value(raw, 6)
        rows = []
        for comp in range(3):
            rows.append(
                predict(value(raw, comp), value(raw, 3 + comp), value(raw, 8 + comp),
                        value(raw, 11 + comp), elapsed)
            )
        return [r[0] for r in rows] + [r[1] for r in rows], elapsed

    def lay_field(step, rows, mass):
        for n, row in enumerate(rows + [mass]):
            field[step, 0:8, n, :] = row
        field[step, 0:8, 7, :] = jnp.zeros((8, LANES), F32)

    rows0, elapsed0 = predicted(STEP)
    for n, row in enumerate(rows0):
        src0[n * 8 : n * 8 + 8, :] = row
    src0[48:56, :] = elapsed0
    src0[56:112, :] = raw[56:112, :]
    lay_field(0, rows0, value(raw, 7))

    sub = lax.broadcasted_iota(jnp.int32, (LANES, LANES), 0)
    sub8 = lax.broadcasted_iota(jnp.int32, (8, LANES), 0)
    first_star = ja * (8 * LANES)

    def high_hot(step, at):
        local = act_v[step : step + 1, pl.ds(at, LANES)] - first_star
        return jnp.right_shift(local, 7) == sub8

    def low_hot_of(step, at):
        lo = jnp.bitwise_and(act_v[step : step + 1, pl.ds(at, LANES)], LANES - 1)
        return jnp.where(lo == sub, 1.0, 0.0).astype(BF16)

    def pick(step, source):
        pieces = split3(source[...])
        for pz in range(zs):
            at = pl.multiple_of(x * quarter + pz * LANES, LANES)
            hot = low_hot_of(step, at)
            got = (dot_nn(pieces[2], hot) + dot_nn(pieces[1], hot)) + dot_nn(pieces[0], hot)
            own = jnp.where(high_hot(step, at)[None], got.reshape(14, 8, LANES), 0.0)
            rows = jnp.concatenate([jnp.sum(own, axis=1), jnp.zeros((2, LANES), F32)], axis=0)
            low, high = rows[0:8], rows[8:16]
            rs_src[step, pz, 0] = jnp.where(low_lanes(), low, swap(high))
            rs_src[step, pz, 1] = jnp.where(low_lanes(), swap(low), high)

    def scatter_picks(step):
        copies = []
        for dz, dc in zc_list:
            pz, pc = lax.rem(z + dz, zs), lax.rem(c + dc, CORES)
            copies.append(
                send(rs_src.at[step, pz, pc], rs_dst.at[step, dz, dc], rs_s.at[step, dz, dc],
                     rs_r.at[step, dz, dc], device(dz, 0, dc, 0))
            )
        return copies

    def reduce_picks(step, copies):
        for copy in copies:
            copy.wait_recv()
        tile = rs_src[step, z, c]
        for dz, dc in zc_list:
            tile = tile + rs_dst[step, dz, dc]
        pick_src[step] = tile
        return [
            send(pick_src.at[step], pick_dst.at[step, dy], pick_s.at[step, dy],
                 pick_r.at[step, dy], device(0, dy, 0, 0))
            for dy in y_list
        ]

    def picked(step, copies):
        for copy in copies:
            copy.wait_recv()
        tile = pick_src[step]
        for dy in y_list:
            tile = tile + pick_dst[step, dy]
        return tile

    block = 8

    def send_field(step):
        copies = []
        for dz in z_list:
            copies.append(
                send(field.at[step, pl.ds(0, block)], field.at[step, pl.ds(dz * block, block)],
                     fz_s.at[step, dz], fz_r.at[step, dz], device(dz, 0, 0, 0))
            )
        across = [forward(step, 0)]
        return copies, across

    def forward(step, dz):
        return send(
            field.at[step, pl.ds(dz * block, block)],
            field.at[step, pl.ds((zs + dz) * block, block)],
            fc_s.at[step, dz], fc_r.at[step, dz], device(0, 0, 1, 0),
        )

    def pass_on(step, copies, across):
        for dz, copy in zip(z_list, copies):
            copy.wait_recv()
            across.append(forward(step, dz))

    def set_columns(tile):
        wide = jnp.concatenate([tile, jnp.zeros((LANES - 8, LANES), F32)], axis=0).T
        for comp in range(6):
            act_cols[comp] = jnp.broadcast_to(wide[0:HALF, comp : comp + 1], (HALF, LANES))

    def forces(step, begin, end, fresh_start):
        def group(g, _):
            rows = pl.ds(pl.multiple_of(g * 8, 8), 8)
            act = [act_cols[comp, rows, :] for comp in range(6)]

            def tile(t, sums):
                parts = [field[step, t, n : n + 1, :] for n in range(7)]
                return pair_terms(act, parts, sums)

            if fresh_start:
                start = tuple(jnp.zeros((8, LANES), F32) for _ in range(6))
            else:
                start = tuple(sums_v[rows, n * LANES : (n + 1) * LANES] for n in range(6))
            done = lax.fori_loop(begin, end, tile, start, unroll=4)
            for n in range(6):
                sums_v[rows, n * LANES : (n + 1) * LANES] = done[n]
            return 0

        lax.fori_loop(0, 8, group, 0)

    def all_sums(step):
        lane = lax.broadcasted_iota(jnp.int32, (8, 6 * LANES), 1)
        row = lax.broadcasted_iota(jnp.int32, (8, 6 * LANES), 0)
        ones = jnp.where(jnp.right_shift(lane, 7) == row, 1.0, 0.0).astype(BF16)
        one, two, three = split3(sums_v[...])
        rows = (dot_nt(ones, three) + dot_nt(ones, two)) + dot_nt(ones, one)
        sum_src[step] = jnp.concatenate([rows, jnp.zeros((8, HALF), F32)], axis=1)
        return [
            send(sum_src.at[step], sum_dst.at[step, y], sum_s.at[step, dy], sum_r.at[step, y],
                 device(0, dy, 0, 0))
            for dy in y_list
        ]

    def total_sums(step, copies):
        sum_dst[step, y] = sum_src[step]
        for dy in y_list:
            other = lax.rem(y + dy, ys)
            pltpu.make_async_remote_copy(
                src_ref=sum_src.at[step], dst_ref=sum_dst.at[step, other],
                send_sem=sum_s.at[step, dy], recv_sem=sum_r.at[step, other],
                device_id=device(0, dy, 0, 0), device_id_type=MESH,
            ).wait_recv()
        tile = sum_dst[step, 0]
        for n in range(1, ys):
            tile = tile + sum_dst[step, n]
        return tile

    def correct(act, force):
        other = swap(act)
        pred_pos, pred_vel, mass = act[0:3], act[3:6], act[7:8]
        elapsed = jnp.where(low_lanes()[0:1], act[6:7], 1.0)
        old_acc, old_jerk = other[0:3], other[3:6]
        new_acc, new_jerk = force[0:3], force[3:6]
        sq = elapsed * elapsed
        diff = old_acc - new_acc
        snap = (-6.0 * diff - elapsed * (4.0 * old_jerk + 2.0 * new_jerk)) / sq
        crackle = (12.0 * diff + 6.0 * elapsed * (old_jerk + new_jerk)) / (sq * elapsed)
        pos = pred_pos + sq * sq / 24.0 * snap + sq * sq * elapsed / 120.0 * crackle
        vel = pred_vel + sq * elapsed / 6.0 * snap + sq * sq / 24.0 * crackle
        one = jnp.ones((1, LANES), F32)
        low = jnp.concatenate([pos, vel, one, mass], axis=0)
        high = jnp.concatenate([new_acc, new_jerk, one, one], axis=0)
        return pack(low, high)

    def gather_fresh(step, tile):
        gath[step, 0, 0, 0] = tile
        copies = {}
        for dz, dx in xz_list:
            copies[dz, dx] = send(
                gath.at[step, 0, 0, 0], gath.at[step, 0, dz, dx], ag_s.at[step, dz, dx],
                ag_r.at[step, dz, dx], device(dz, 0, 0, dx),
            )
        return copies

    def finish_gather(step, copies):
        across = []
        for dz in [0] + z_list:
            for dx in range(xs):
                if (dz, dx) != (0, 0):
                    copies[dz, dx].wait_recv()
            across.append(
                send(gath.at[step, 0, dz], gath.at[step, 1, dz], agc_s.at[step, dz],
                     agc_r.at[step, dz], device(0, 0, 1, 0))
            )
        for copy in across:
            copy.wait_recv()
        for px in range(xs):
            for pz in range(zs):
                dz, dx = lax.rem(z - pz + zs, zs), lax.rem(x - px + xs, xs)
                tile0 = gath[step, c, dz, dx]
                tile1 = gath[step, 1 - c, dz, dx]
                at = (px * zs + pz) * LANES
                corr[step, 0:8, at : at + LANES] = jnp.where(low_lanes(), tile0, swap(tile1))
                corr[step, 8:16, at : at + LANES] = jnp.where(low_lanes(), swap(tile0), tile1)

    chunks = total // LANES

    def build_low_hot(step):
        def one(n, _):
            at = pl.multiple_of(n * LANES, LANES)
            low_hot[step, :, pl.ds(at, LANES)] = low_hot_of(step, at)
            return 0

        lax.fori_loop(0, chunks, one, 0)

    def hits(step):
        def one(n, seen):
            at = pl.multiple_of(n * LANES, LANES)
            hot = jnp.where(high_hot(step, at), 1.0, 0.0).astype(BF16)
            return seen + dot_nt(hot, low_hot[step, :, pl.ds(at, LANES)])

        return lax.fori_loop(0, chunks, one, jnp.zeros((8, LANES), F32))

    def build_match():
        at = pl.multiple_of(x * quarter + z * LANES, LANES)
        mine = act_v[1:2, pl.ds(at, LANES)].astype(F32)
        column[...] = jnp.broadcast_to(mine, (LANES, LANES)).T
        own = column[pl.ds(pl.multiple_of(c * HALF, HALF), HALF), :]

        def one(n, _):
            at = pl.multiple_of(n * LANES, LANES)
            row = act_v[0:1, pl.ds(at, LANES)].astype(F32)
            match[:, pl.ds(at, LANES)] = jnp.where(own == row, 1.0, 0.0).astype(BF16)
            return 0

        lax.fori_loop(0, chunks, one, 0)

    def place(step, hit):
        names = [0, 1, 2, 3, 4, 5, 8, 9, 10, 11, 12, 13]

        def one(n, done):
            at = pl.multiple_of(n * LANES, LANES)
            mine = high_hot(step, at)
            rows = [
                jnp.where(mine, corr[step, v : v + 1, pl.ds(at, LANES)], 0.0) for v in names
            ]
            left = jnp.concatenate(rows, axis=0)
            return done + exact_nt(left, low_hot[step, :, pl.ds(at, LANES)])

        scat[...] = lax.fori_loop(0, chunks, one, jnp.zeros((96, LANES), F32))
        taken = hit > 0.5
        for n, v in enumerate(names):
            at = v * 8
            raw[at : at + 8, :] = jnp.where(taken, scat[n * 8 : n * 8 + 8, :], raw[at : at + 8, :])
        raw[48:56, :] = jnp.where(taken, STEP * (step + 1), raw[48:56, :])

    def write_state(step):
        state_out[step, 0:6, :] = corr[step, 0:6, :]
        state_out[step, 6:12, :] = corr[step, 8:14, :]

    pick(0, src0)
    pl.semaphore_wait(barrier, len(partners))
    rs0 = scatter_picks(0)
    f0, across0 = send_field(0)
    pick(1, raw)
    rs1 = scatter_picks(1)
    build_low_hot(0)
    hit0 = hits(0)
    fresh[0] = hit0
    rows1, _ = predicted(2 * STEP)
    lay_field(1, rows1, jnp.where(hit0 > 0.5, 0.0, value(raw, 7)))
    ar0 = reduce_picks(0, rs0)
    f1, across1 = send_field(1)
    pass_on(0, f0, across0)
    ar1 = reduce_picks(1, rs1)
    act0 = picked(0, ar0)
    set_columns(act0)
    forces(0, 0, zs * block, True)
    for copy in across0:
        copy.wait_recv()
    forces(0, zs * block, 2 * zs * block, False)
    s0 = all_sums(0)
    pass_on(1, f1, across1)
    act1_raw = picked(1, ar1)
    build_match()
    force0 = total_sums(0, s0)
    fresh0 = gather_fresh(0, correct(act0, force0))
    build_low_hot(1)
    fresh[1] = hits(1)
    for copy in across1:
        copy.wait_recv()
    finish_gather(0, fresh0)

    extra = total // ys
    for n in range(extra // LANES):
        at = pl.multiple_of(y * extra + n * LANES, LANES)
        low = corr[0, 0:8, pl.ds(at, LANES)]
        high = corr[0, 8:16, pl.ds(at, LANES)]
        new_pos, new_vel = predict(low[0:3], low[3:6], high[0:3], high[3:6], 2 * STEP - STEP)
        field[1, 2 * zs * block + n] = jnp.concatenate(
            [new_pos, new_vel, low[7:8], jnp.zeros((1, LANES), F32)], axis=0
        )
    found = exact_nt(corr[0], match[...])
    found = jnp.concatenate([found, jnp.zeros((16, HALF), F32)], axis=1)
    again = found[14:15] > 0.5
    low = jnp.where(again, found[0:8], act1_raw)
    high = jnp.where(again, found[8:16], swap(act1_raw))
    last = jnp.where(again, STEP, act1_raw[6:7])
    elapsed1 = 2 * STEP - last
    pos1, vel1 = predict(low[0:3], low[3:6], high[0:3], high[3:6], elapsed1)
    act1 = pack(jnp.concatenate([pos1, vel1, elapsed1, low[7:8]], axis=0), high)
    set_columns(act1)
    forces(1, 0, 2 * zs * block + extra // LANES, True)
    s1 = all_sums(1)
    place(0, fresh[0])
    write_state(0)
    force1 = total_sums(1, s1)
    fresh1 = gather_fresh(1, correct(act1, force1))
    finish_gather(1, fresh1)
    place(1, fresh[1])
    write_state(1)
    for ref, at in ((pos_out, 0), (vel_out, 3), (acc_out, 8), (jerk_out, 11)):
        for comp in range(3):
            for hi in range(8):
                row = (at + comp) * 8 + hi
                ref[comp : comp + 1, hi * LANES : (hi + 1) * LANES] = raw[row : row + 1, :]
    time_out[...] = raw[48:56, :]
    for copy in started:
        copy.wait_send()


def run(sizes, *args):
    zs, ys, xs = sizes
    total = xs * zs * LANES
    vmem = pltpu.VMEM
    dma = pltpu.SemaphoreType.DMA
    tiles = 2 * zs * 8 + total // ys // LANES
    scratch = [
        vmem((3, 1024), F32), vmem((3, 1024), F32), vmem((3, 1024), F32), vmem((3, 1024), F32),
        vmem((8, LANES), F32), vmem((8, LANES), F32), vmem((2, total), jnp.int32),
        vmem((112, LANES), F32), vmem((112, LANES), F32),
        vmem((2, zs, CORES, 8, LANES), F32), vmem((2, zs, CORES, 8, LANES), F32),
        vmem((2, 8, LANES), F32), vmem((2, ys, 8, LANES), F32),
        vmem((2, 8, LANES), F32), vmem((2, ys, 8, LANES), F32),
        vmem((2, tiles, 8, LANES), F32),
        vmem((2, CORES, zs, xs, 8, LANES), F32),
        vmem((6, HALF, LANES), F32), vmem((HALF, 6 * LANES), F32),
        vmem((2, 16, total), F32), vmem((2, LANES, total), BF16), vmem((HALF, total), BF16),
        vmem((LANES, LANES), F32), vmem((96, LANES), F32), vmem((2, 8, LANES), F32),
        dma((7,)),
        dma((2, zs, CORES)), dma((2, zs, CORES)),
        dma((2, ys)), dma((2, ys)), dma((2, ys)), dma((2, ys)),
        dma((2, zs)), dma((2, zs)), dma((2, zs)), dma((2, zs)),
        dma((2, zs, xs)), dma((2, zs, xs)), dma((2, zs)), dma((2, zs)),
    ]
    flat = jax.ShapeDtypeStruct((3, 1024), F32)
    out_shape = [flat, flat, flat, flat, jax.ShapeDtypeStruct((8, LANES), F32),
                 jax.ShapeDtypeStruct((2, 12, total), F32)]
    return pl.pallas_call(
        functools.partial(kernel, sizes),
        out_shape=out_shape,
        in_specs=[pl.BlockSpec(memory_space=pl.ANY)] * 7,
        out_specs=[pl.BlockSpec(memory_space=pltpu.VMEM)] * 6,
        scratch_shapes=scratch,
        compiler_params=pltpu.CompilerParams(
            collective_id=0, has_side_effects=True, vmem_limit_bytes=48 << 20
        ),
        name="hermite",
    )(*args)


def per_device(sizes, positions, velocities, accels, jerks, masses, last_time, active):
    pos, vel, acc, jerk, times, state = run(
        sizes, positions, velocities, accels, jerks,
        masses.reshape(8, LANES), last_time.reshape(8, LANES), active,
    )
    return pos, vel, acc, jerk, times.reshape(8 * LANES), state


def solution(mesh, sizes=(RINGS["z"], RINGS["y"], RINGS["x"])):
    in_specs = (P(None, "ja"), P(None, "ja"), P(None, "ja"), P(None, "ja"), P("ja"), P("ja"), P())
    out_specs = (P(None, "ja"), P(None, "ja"), P(None, "ja"), P(None, "ja"), P("ja"), P())
    return jax.shard_map(
        functools.partial(per_device, sizes), mesh=mesh, in_specs=in_specs, out_specs=out_specs,
        check_vma=False,
    )
```

time: 2410 us -> 90.4 us (0.04)
  blocking collectives: 2190 us -> 0 us
  local copies, waits for them, and re-layouts: 186 us -> 9.05 us
  Pallas kernels: 0 us -> 80.1 us
  other arithmetic: 26.2 us -> 0 us
    psum x2 -> x0, blocking collectives: 987 us -> none  [per_device(): act_rows = lax.psum(picked, 'ja')]
    unnamed x2 -> x0, blocking collectives: 982 us -> none
    all_gather x2 -> x0, blocking collectives: 225 us -> none  [per_device(): gathered = lax.all_gather(fresh_rows, ('ja', 'ia'), axis=1, tiled=True)]
    scatter x14 -> x0, local copies, waits for them, and re-layouts: 121 us -> none  [the longest x2 31 us: per_device(): last_time.at[target]]
    pallas_call x0 -> x1, Pallas kernels: none -> 80.1 us  [run(): pl.pallas_call(functools.partial(kernel, sizes), out_shape=out_shape, in_...]
    slice x21 -> x0, local copies, waits for them, and re-layouts: 30.6 us -> none  [the longest x6 9.27 us: per_device(): jerks = jerks.at[:, target].set(corrected[9:12], mode='drop')]
where the time goes in v1:
time: 90.4 us; the launch traced here: 89.8 us
  Pallas kernels  80.1 us (89%)
  local copies, waits for them, and re-layouts  9.05 us (10%)
    pallas_call x1, Pallas kernels, run(): pl.pallas_call(functools.partial(kernel, sizes), out_shape=out_shape, in_...  80.1 us
    unnamed x20, local copies, waits for them, and re-layouts  9.05 us

profile of v1, /device:TPU:1, one launch (start us, length us, event | category | flops | bytes accessed | tf_op | source)
XLA Modules:
  0.0 89.8 jit_solution(875990105786000133)
XLA Ops:
  0.6 0.0 copy-start
  0.6 0.7 copy-done
  1.4 0.0 copy-start.1
  1.4 0.7 copy-done.1
  2.1 0.0 copy-start.2
  2.1 0.7 copy-done.2
  2.8 0.0 copy-start.3
  2.8 0.7 copy-done.3
  3.5 0.0 copy-start.4
  3.5 0.7 copy-done.4
  4.3 0.0 copy-start.5
  4.3 0.7 copy-done.5
  5.0 0.0 copy-start.6
  5.0 0.7 copy-done.6
  5.6 80.1 %hermite.1 = (f32[3,1024]{1,0:T(4,128)S(1)}, f32[3,1024]{1,0:T(4,128)S(1)}, f32[3,1024]{1,0:T(4,128)S(1)}, f32[3,1024]{1,0:T(4,128)S(1)}, f32[8,128]{1,0:T(8,128)S(1)}, /*index=5*/f32[2,12,4096]{2,1,0:T(8,128)S(1)}) custom-call(f32[3,1024]{1,0:T(4,128)S(1)} %copy-done.1, f32[3,1024]{1,0:T(4,128)S(1)} %copy-done.2, f32[3,1024]{1,0:T(4,128)S(1)} %copy-done.3, ...), custom_call_target="tpu_custom_call" | custom-call | tf_op jit(solution)/shard_map/hermite/pallas_call | solution.py:518
  85.8 1.1 %copy.13 = f32[2,12,4096]{2,0,1:T(2,128)} copy(f32[2,12,4096]{2,1,0:T(8,128)S(1)} %get-tuple-element.23) | data formatting | bytes 786432
  86.8 0.6 copy.19
  87.4 0.6 copy.20
  88.0 0.6 copy.21
  88.6 0.6 copy.22
  89.2 0.6 copy.23
Async XLA Ops:
  0.6 0.8 copy-start
  1.4 0.7 copy-start.1
  2.1 0.7 copy-start.2
  2.8 0.7 copy-start.3
  3.5 0.7 copy-start.4
  4.3 0.7 copy-start.5
  5.0 0.7 copy-start.6

commit v2 on v1

--- a/solution.py
+++ b/solution.py
@@ -92,7 +92,7 @@
     pos_out, vel_out, acc_out, jerk_out, time_out, state_out,
     pos_v, vel_v, acc_v, jerk_v, mass_v, last_v, act_v,
     raw, src0, rs_src, rs_dst, pick_src, pick_dst, sum_src, sum_dst,
-    field, gath, act_cols, sums_v, corr, low_hot, match, column, scat, fresh,
+    field, gath, act_cols, sums_v, corr, low_hot, match, column, scat, fresh, left, state_v, time_v, out_sem,
     in_sem, rs_s, rs_r, pick_s, pick_r, sum_s, sum_r, fz_s, fz_r, fc_s, fc_r,
     ag_s, ag_r, agc_s, agc_r,
 ):
@@ -363,6 +363,7 @@
                 corr[step, 8:16, at : at + LANES] = jnp.where(low_lanes(), swap(tile0), tile1)
 
     chunks = total // LANES
+    names = [0, 1, 2, 3, 4, 5, 8, 9, 10, 11, 12, 13]
 
     def build_low_hot(step):
         def one(n, _):
@@ -373,12 +374,14 @@
         lax.fori_loop(0, chunks, one, 0)
 
     def hits(step):
-        def one(n, seen):
+        def one(n, _):
             at = pl.multiple_of(n * LANES, LANES)
-            hot = jnp.where(high_hot(step, at), 1.0, 0.0).astype(BF16)
-            return seen + dot_nt(hot, low_hot[step, :, pl.ds(at, LANES)])
-
-        return lax.fori_loop(0, chunks, one, jnp.zeros((8, LANES), F32))
+            hot = jnp.where(high_hot(step, at), 1.0, 0.0)
+            left[0:16, pl.ds(at, LANES)] = jnp.concatenate([hot, hot], axis=0).astype(BF16)
+            return 0
+
+        lax.fori_loop(0, chunks, one, 0, unroll=2)
+        return dot_nt(left[0:16, :], low_hot[step])[0:8]
 
     def build_match():
         at = pl.multiple_of(x * quarter + z * LANES, LANES)
@@ -395,18 +398,19 @@
         lax.fori_loop(0, chunks, one, 0)
 
     def place(step, hit):
-        names = [0, 1, 2, 3, 4, 5, 8, 9, 10, 11, 12, 13]
-
-        def one(n, done):
+        def one(n, _):
             at = pl.multiple_of(n * LANES, LANES)
             mine = high_hot(step, at)
-            rows = [
-                jnp.where(mine, corr[step, v : v + 1, pl.ds(at, LANES)], 0.0) for v in names
-            ]
-            left = jnp.concatenate(rows, axis=0)
-            return done + exact_nt(left, low_hot[step, :, pl.ds(at, LANES)])
-
-        scat[...] = lax.fori_loop(0, chunks, one, jnp.zeros((96, LANES), F32))
+            pieces = split3(corr[step, :, pl.ds(at, LANES)])
+            for p, piece in enumerate(pieces):
+                wide = piece.astype(F32)
+                rows = [jnp.where(mine, wide[v : v + 1], 0.0) for v in names]
+                left[p * 96 : p * 96 + 96, pl.ds(at, LANES)] = jnp.concatenate(rows, axis=0).astype(BF16)
+            return 0
+
+        lax.fori_loop(0, chunks, one, 0, unroll=2)
+        got = dot_nt(left[...], low_hot[step])
+        scat[...] = (got[192:288] + got[96:192]) + got[0:96]
         taken = hit > 0.5
         for n, v in enumerate(names):
             at = v * 8
@@ -414,8 +418,8 @@
         raw[48:56, :] = jnp.where(taken, STEP * (step + 1), raw[48:56, :])
 
     def write_state(step):
-        state_out[step, 0:6, :] = corr[step, 0:6, :]
-        state_out[step, 6:12, :] = corr[step, 8:14, :]
+        for n, v in enumerate(names):
+            state_v[n, step : step + 1, :] = corr[step, v : v + 1, :]
 
     pick(0, src0)
     pl.semaphore_wait(barrier, len(partners))
@@ -476,16 +480,34 @@
     force1 = total_sums(1, s1)
     fresh1 = gather_fresh(1, correct(act1, force1))
     finish_gather(1, fresh1)
+    write_state(1)
+    stores = [pltpu.make_async_copy(state_v, state_out, out_sem.at[5])]
+    stores[0].start()
     place(1, fresh[1])
-    write_state(1)
-    for ref, at in ((pos_out, 0), (vel_out, 3), (acc_out, 8), (jerk_out, 11)):
+    for ref, at in ((pos_v, 0), (vel_v, 3), (acc_v, 8), (jerk_v, 11)):
         for comp in range(3):
             for hi in range(8):
                 row = (at + comp) * 8 + hi
                 ref[comp : comp + 1, hi * LANES : (hi + 1) * LANES] = raw[row : row + 1, :]
-    time_out[...] = raw[48:56, :]
+    time_v[...] = raw[48:56, :]
+    for n, (a, b) in enumerate(
+        [(pos_v, pos_out), (vel_v, vel_out), (acc_v, acc_out), (jerk_v, jerk_out), (time_v, time_out)]
+    ):
+        stores.append(pltpu.make_async_copy(a, b, out_sem.at[n]))
+        stores[-1].start()
     for copy in started:
         copy.wait_send()
+    for store in stores:
+        store.wait()
+
+
+def hand_on(*refs):
+    srcs, dsts, sem = refs[0:6], refs[6:12], refs[12]
+    copies = [pltpu.make_async_copy(a, b, sem.at[n]) for n, (a, b) in enumerate(zip(srcs, dsts))]
+    for copy in copies:
+        copy.start()
+    for copy in copies:
+        copy.wait()
 
 
 def run(sizes, *args):
@@ -506,6 +528,7 @@
         vmem((6, HALF, LANES), F32), vmem((HALF, 6 * LANES), F32),
         vmem((2, 16, total), F32), vmem((2, LANES, total), BF16), vmem((HALF, total), BF16),
         vmem((LANES, LANES), F32), vmem((96, LANES), F32), vmem((2, 8, LANES), F32),
+        vmem((288, total), BF16), vmem((12, 2, total), F32), vmem((8, LANES), F32), dma((6,)),
         dma((7,)),
         dma((2, zs, CORES)), dma((2, zs, CORES)),
         dma((2, ys)), dma((2, ys)), dma((2, ys)), dma((2, ys)),
@@ -514,18 +537,27 @@
     ]
     flat = jax.ShapeDtypeStruct((3, 1024), F32)
     out_shape = [flat, flat, flat, flat, jax.ShapeDtypeStruct((8, LANES), F32),
-                 jax.ShapeDtypeStruct((2, 12, total), F32)]
-    return pl.pallas_call(
+                 jax.ShapeDtypeStruct((12, 2, total), F32)]
+    results = pl.pallas_call(
         functools.partial(kernel, sizes),
         out_shape=out_shape,
         in_specs=[pl.BlockSpec(memory_space=pl.ANY)] * 7,
-        out_specs=[pl.BlockSpec(memory_space=pltpu.VMEM)] * 6,
+        out_specs=[pl.BlockSpec(memory_space=pl.ANY)] * 6,
         scratch_shapes=scratch,
         compiler_params=pltpu.CompilerParams(
-            collective_id=0, has_side_effects=True, vmem_limit_bytes=48 << 20
+            collective_id=0, has_side_effects=True, vmem_limit_bytes=62 << 20
         ),
         name="hermite",
     )(*args)
+    return pl.pallas_call(
+        hand_on,
+        out_shape=out_shape,
+        in_specs=[pl.BlockSpec(memory_space=pl.ANY)] * 6,
+        out_specs=[pl.BlockSpec(memory_space=pl.ANY)] * 6,
+        scratch_shapes=[dma((6,))],
+        compiler_params=pltpu.CompilerParams(vmem_limit_bytes=62 << 20),
+        name="finish",
+    )(*results)
 
 
 def per_device(sizes, positions, velocities, accels, jerks, masses, last_time, active):
@@ -533,7 +565,7 @@
         sizes, positions, velocities, accels, jerks,
         masses.reshape(8, LANES), last_time.reshape(8, LANES), active,
     )
-    return pos, vel, acc, jerk, times.reshape(8 * LANES), state
+    return pos, vel, acc, jerk, times.reshape(8 * LANES), state.transpose(1, 0, 2)
 
 
 def solution(mesh, sizes=(RINGS["z"], RINGS["y"], RINGS["x"])):

time: 90.4 us -> 89.6 us (level)
  local copies, waits for them, and re-layouts: 9.05 us -> 0 us
  Pallas kernels: 80.1 us -> 88.8 us
    pallas_call x0 -> x1, Pallas kernels: none -> 15.2 us  [run(): pl.pallas_call(hand_on, out_shape=out_shape, in_specs=[pl.BlockSpec(memor...]
    unnamed x20 -> x0, local copies, waits for them, and re-layouts: 9.05 us -> none
    pallas_call x1, Pallas kernels: 80.1 us -> 73.6 us  [run(): pl.pallas_call(functools.partial(kernel, sizes), out_shape=out_shape, in_...]
where the time goes in v2:
time: 89.6 us; the launch traced here: 89.4 us
  Pallas kernels  88.8 us (99%)
    pallas_call x1, Pallas kernels, run(): pl.pallas_call(functools.partial(kernel, sizes), out_shape=out_shape, in_...  73.6 us
    pallas_call x1, Pallas kernels, run(): pl.pallas_call(hand_on, out_shape=out_shape, in_specs=[pl.BlockSpec(memor...  15.2 us

profile of v2, /device:TPU:1, one launch (start us, length us, event | category | flops | bytes accessed | tf_op | source)
XLA Modules:
  0.0 89.4 jit_solution(5729125318966238734)
XLA Ops:
  0.6 73.6 %hermite.1 = (f32[3,1024]{1,0:T(4,128)}, f32[3,1024]{1,0:T(4,128)}, f32[3,1024]{1,0:T(4,128)}, f32[3,1024]{1,0:T(4,128)}, f32[8,128]{1,0:T(8,128)}, /*index=5*/f32[12,2,4096]{2,1,0:T(2,128)}) custom-call(f32[3,1024]{1,0:T(4,128)} %pos_in.1, f32[3,1024]{1,0:T(4,128)} %vel_in.1, f32[3,1024]{1,0:T(4,128)} %acc_in.1, f32[3,1024]{1,0:T(4,128)} %jerk_in.1, ...), custom_call_target="tpu_custom_call" | custom-call | tf_op jit(solution)/shard_map/hermite/pallas_call | solution.py:541
  74.2 15.2 %finish.1 = (f32[3,1024]{1,0:T(4,128)}, f32[3,1024]{1,0:T(4,128)}, f32[3,1024]{1,0:T(4,128)}, f32[3,1024]{1,0:T(4,128)}, f32[8,128]{1,0:T(8,128)}, /*index=5*/f32[12,2,4096]{2,1,0:T(2,128)}) custom-call(f32[3,1024]{1,0:T(4,128)} %get-tuple-element.18.refs_0_, f32[3,1024]{1,0:T(4,128)} %get-tuple-element.19.refs_1_, f32[3,1024]{1,0:T(4,128)} %get-tuple-element.20.refs_2_, ...), custom_call_target="tpu_custom_call" | custom-call | tf_op jit(solution)/shard_map/finish/pallas_call | solution.py:552

commit v3 on v2

--- a/solution.py
+++ b/solution.py
@@ -502,12 +502,16 @@
 
 
 def hand_on(*refs):
-    srcs, dsts, sem = refs[0:6], refs[6:12], refs[12]
-    copies = [pltpu.make_async_copy(a, b, sem.at[n]) for n, (a, b) in enumerate(zip(srcs, dsts))]
-    for copy in copies:
-        copy.start()
-    for copy in copies:
-        copy.wait()
+    srcs, dsts, held, sem = refs[0:6], refs[6:12], refs[12:18], refs[18]
+    loads = [pltpu.make_async_copy(a, b, sem.at[0, n]) for n, (a, b) in enumerate(zip(srcs, held))]
+    stores = [pltpu.make_async_copy(a, b, sem.at[1, n]) for n, (a, b) in enumerate(zip(held, dsts))]
+    for load in loads:
+        load.start()
+    for load, store in zip(loads, stores):
+        load.wait()
+        store.start()
+    for store in stores:
+        store.wait()
 
 
 def run(sizes, *args):
@@ -554,7 +558,7 @@
         out_shape=out_shape,
         in_specs=[pl.BlockSpec(memory_space=pl.ANY)] * 6,
         out_specs=[pl.BlockSpec(memory_space=pl.ANY)] * 6,
-        scratch_shapes=[dma((6,))],
+        scratch_shapes=[vmem(out.shape, F32) for out in out_shape] + [dma((2, 6))],
         compiler_params=pltpu.CompilerParams(vmem_limit_bytes=62 << 20),
         name="finish",
     )(*results)

time: 89.6 us -> 76.4 us (0.85)
  Pallas kernels: 88.8 us -> 75.5 us
    pallas_call x1, Pallas kernels: 15.2 us -> 1.92 us  [run(): pl.pallas_call(hand_on, out_shape=out_shape, in_specs=[pl.BlockSpec(memor...]
where the time goes in v3:
time: 76.4 us; the launch traced here: 76.1 us
  Pallas kernels  75.5 us (99%)
    pallas_call x1, Pallas kernels, run(): pl.pallas_call(functools.partial(kernel, sizes), out_shape=out_shape, in_...  73.6 us
    pallas_call x1, Pallas kernels, run(): pl.pallas_call(hand_on, out_shape=out_shape, in_specs=[pl.BlockSpec(memor...  1.92 us

profile of v3, /device:TPU:1, one launch (start us, length us, event | category | flops | bytes accessed | tf_op | source)
XLA Modules:
  0.0 76.1 jit_solution(13655803861426209649)
XLA Ops:
  0.6 73.6 %hermite.1 = (f32[3,1024]{1,0:T(4,128)}, f32[3,1024]{1,0:T(4,128)}, f32[3,1024]{1,0:T(4,128)}, f32[3,1024]{1,0:T(4,128)}, f32[8,128]{1,0:T(8,128)}, /*index=5*/f32[12,2,4096]{2,1,0:T(2,128)}) custom-call(f32[3,1024]{1,0:T(4,128)} %pos_in.1, f32[3,1024]{1,0:T(4,128)} %vel_in.1, f32[3,1024]{1,0:T(4,128)} %acc_in.1, f32[3,1024]{1,0:T(4,128)} %jerk_in.1, ...), custom_call_target="tpu_custom_call" | custom-call | tf_op jit(solution)/shard_map/hermite/pallas_call | solution.py:545
  74.2 1.9 %finish.1 = (f32[3,1024]{1,0:T(4,128)}, f32[3,1024]{1,0:T(4,128)}, f32[3,1024]{1,0:T(4,128)}, f32[3,1024]{1,0:T(4,128)}, f32[8,128]{1,0:T(8,128)}, /*index=5*/f32[12,2,4096]{2,1,0:T(2,128)}) custom-call(f32[3,1024]{1,0:T(4,128)} %get-tuple-element.18.refs_0_, f32[3,1024]{1,0:T(4,128)} %get-tuple-element.19.refs_1_, f32[3,1024]{1,0:T(4,128)} %get-tuple-element.20.refs_2_, ...), custom_call_target="tpu_custom_call" | custom-call | tf_op jit(solution)/shard_map/finish/pallas_call | solution.py:556

commit v4 on v2

--- a/solution.py
+++ b/solution.py
@@ -92,7 +92,7 @@
     pos_out, vel_out, acc_out, jerk_out, time_out, state_out,
     pos_v, vel_v, acc_v, jerk_v, mass_v, last_v, act_v,
     raw, src0, rs_src, rs_dst, pick_src, pick_dst, sum_src, sum_dst,
-    field, gath, act_cols, sums_v, corr, low_hot, match, column, scat, fresh, left, state_v, time_v, out_sem,
+    field, gath, act_cols, sums_v, corr, low_hot, match, column, scat, fresh, left,
     in_sem, rs_s, rs_r, pick_s, pick_r, sum_s, sum_r, fz_s, fz_r, fc_s, fc_r,
     ag_s, ag_r, agc_s, agc_r,
 ):
@@ -280,7 +280,7 @@
                 start = tuple(jnp.zeros((8, LANES), F32) for _ in range(6))
             else:
                 start = tuple(sums_v[rows, n * LANES : (n + 1) * LANES] for n in range(6))
-            done = lax.fori_loop(begin, end, tile, start, unroll=4)
+            done = lax.fori_loop(begin, end, tile, start, unroll=16)
             for n in range(6):
                 sums_v[rows, n * LANES : (n + 1) * LANES] = done[n]
             return 0
@@ -419,37 +419,37 @@
 
     def write_state(step):
         for n, v in enumerate(names):
-            state_v[n, step : step + 1, :] = corr[step, v : v + 1, :]
+            state_out[n, step : step + 1, :] = corr[step, v : v + 1, :]
 
     pick(0, src0)
     pl.semaphore_wait(barrier, len(partners))
     rs0 = scatter_picks(0)
     f0, across0 = send_field(0)
     pick(1, raw)
-    rs1 = scatter_picks(1)
     build_low_hot(0)
+    ar0 = reduce_picks(0, rs0)
     hit0 = hits(0)
     fresh[0] = hit0
     rows1, _ = predicted(2 * STEP)
     lay_field(1, rows1, jnp.where(hit0 > 0.5, 0.0, value(raw, 7)))
-    ar0 = reduce_picks(0, rs0)
+    pass_on(0, f0, across0)
+    act0 = picked(0, ar0)
+    rs1 = scatter_picks(1)
     f1, across1 = send_field(1)
-    pass_on(0, f0, across0)
-    ar1 = reduce_picks(1, rs1)
-    act0 = picked(0, ar0)
     set_columns(act0)
     forces(0, 0, zs * block, True)
     for copy in across0:
         copy.wait_recv()
     forces(0, zs * block, 2 * zs * block, False)
     s0 = all_sums(0)
-    pass_on(1, f1, across1)
-    act1_raw = picked(1, ar1)
+    ar1 = reduce_picks(1, rs1)
     build_match()
     force0 = total_sums(0, s0)
     fresh0 = gather_fresh(0, correct(act0, force0))
+    pass_on(1, f1, across1)
     build_low_hot(1)
     fresh[1] = hits(1)
+    act1_raw = picked(1, ar1)
     for copy in across1:
         copy.wait_recv()
     finish_gather(0, fresh0)
@@ -481,33 +481,24 @@
     fresh1 = gather_fresh(1, correct(act1, force1))
     finish_gather(1, fresh1)
     write_state(1)
-    stores = [pltpu.make_async_copy(state_v, state_out, out_sem.at[5])]
-    stores[0].start()
     place(1, fresh[1])
-    for ref, at in ((pos_v, 0), (vel_v, 3), (acc_v, 8), (jerk_v, 11)):
+    for ref, at in ((pos_out, 0), (vel_out, 3), (acc_out, 8), (jerk_out, 11)):
         for comp in range(3):
             for hi in range(8):
                 row = (at + comp) * 8 + hi
                 ref[comp : comp + 1, hi * LANES : (hi + 1) * LANES] = raw[row : row + 1, :]
-    time_v[...] = raw[48:56, :]
-    for n, (a, b) in enumerate(
-        [(pos_v, pos_out), (vel_v, vel_out), (acc_v, acc_out), (jerk_v, jerk_out), (time_v, time_out)]
-    ):
-        stores.append(pltpu.make_async_copy(a, b, out_sem.at[n]))
-        stores[-1].start()
+    time_out[...] = raw[48:56, :]
     for copy in started:
         copy.wait_send()
+
+
+def hand_on(*refs):
+    srcs, dsts, sem = refs[0:6], refs[6:12], refs[12]
+    stores = [pltpu.make_async_copy(a, b, sem.at[n]) for n, (a, b) in enumerate(zip(srcs, dsts))]
+    for store in reversed(stores):
+        store.start()
     for store in stores:
         store.wait()
-
-
-def hand_on(*refs):
-    srcs, dsts, sem = refs[0:6], refs[6:12], refs[12]
-    copies = [pltpu.make_async_copy(a, b, sem.at[n]) for n, (a, b) in enumerate(zip(srcs, dsts))]
-    for copy in copies:
-        copy.start()
-    for copy in copies:
-        copy.wait()
 
 
 def run(sizes, *args):
@@ -528,7 +519,7 @@
         vmem((6, HALF, LANES), F32), vmem((HALF, 6 * LANES), F32),
         vmem((2, 16, total), F32), vmem((2, LANES, total), BF16), vmem((HALF, total), BF16),
         vmem((LANES, LANES), F32), vmem((96, LANES), F32), vmem((2, 8, LANES), F32),
-        vmem((288, total), BF16), vmem((12, 2, total), F32), vmem((8, LANES), F32), dma((6,)),
+        vmem((288, total), BF16),
         dma((7,)),
         dma((2, zs, CORES)), dma((2, zs, CORES)),
         dma((2, ys)), dma((2, ys)), dma((2, ys)), dma((2, ys)),
@@ -538,24 +529,25 @@
     flat = jax.ShapeDtypeStruct((3, 1024), F32)
     out_shape = [flat, flat, flat, flat, jax.ShapeDtypeStruct((8, LANES), F32),
                  jax.ShapeDtypeStruct((12, 2, total), F32)]
+    args = [pltpu.with_memory_space_constraint(arg, pltpu.HBM) for arg in args]
     results = pl.pallas_call(
         functools.partial(kernel, sizes),
-        out_shape=out_shape,
-        in_specs=[pl.BlockSpec(memory_space=pl.ANY)] * 7,
-        out_specs=[pl.BlockSpec(memory_space=pl.ANY)] * 6,
+        out_shape=[pltpu.VMEM(out.shape, F32) for out in out_shape],
+        in_specs=[pl.BlockSpec(memory_space=pltpu.HBM)] * 7,
+        out_specs=[pl.BlockSpec(memory_space=pltpu.VMEM)] * 6,
         scratch_shapes=scratch,
         compiler_params=pltpu.CompilerParams(
-            collective_id=0, has_side_effects=True, vmem_limit_bytes=62 << 20
+            collective_id=0, has_side_effects=True, vmem_limit_bytes=40 << 20
         ),
         name="hermite",
     )(*args)
     return pl.pallas_call(
         hand_on,
         out_shape=out_shape,
-        in_specs=[pl.BlockSpec(memory_space=pl.ANY)] * 6,
+        in_specs=[pl.BlockSpec(memory_space=pltpu.VMEM)] * 6,
         out_specs=[pl.BlockSpec(memory_space=pl.ANY)] * 6,
         scratch_shapes=[dma((6,))],
-        compiler_params=pltpu.CompilerParams(vmem_limit_bytes=62 << 20),
+        compiler_params=pltpu.CompilerParams(vmem_limit_bytes=40 << 20),
         name="finish",
     )(*results)
 

time: 89.6 us -> 71.6 us (0.80)
  Pallas kernels: 88.8 us -> 70.8 us
    pallas_call x1, Pallas kernels: 15.2 us -> 0.82 us  [run(): pl.pallas_call(hand_on, out_shape=out_shape, in_specs=[pl.BlockSpec(memor...]
    pallas_call x1, Pallas kernels: 73.6 us -> 70 us  [run(): pl.pallas_call(functools.partial(kernel, sizes), out_shape=[pltpu.VMEM(ou...]
where the time goes in v4:
time: 71.6 us; the launch traced here: 71.4 us
  Pallas kernels  70.8 us (99%)
    pallas_call x1, Pallas kernels, run(): pl.pallas_call(functools.partial(kernel, sizes), out_shape=[pltpu.VMEM(ou...  70 us

profile of v4, /device:TPU:1, one launch (start us, length us, event | category | flops | bytes accessed | tf_op | source)
XLA Modules:
  0.0 71.4 jit_solution(3230877241644119880)
XLA Ops:
  0.6 70.0 %hermite.1 = (f32[3,1024]{1,0:T(4,128)S(1)}, f32[3,1024]{1,0:T(4,128)S(1)}, f32[3,1024]{1,0:T(4,128)S(1)}, f32[3,1024]{1,0:T(4,128)S(1)}, f32[8,128]{1,0:T(8,128)S(1)}, /*index=5*/f32[12,2,4096]{2,1,0:T(2,128)S(1)}) custom-call(f32[3,1024]{1,0:T(4,128)} %pos_in.1, f32[3,1024]{1,0:T(4,128)} %vel_in.1, f32[3,1024]{1,0:T(4,128)} %acc_in.1, f32[3,1024]{1,0:T(4,128)} %jerk_in.1, ...), custom_call_target="tpu_custom_call" | custom-call | tf_op jit(solution)/shard_map/hermite/pallas_call | solution.py:533
  70.6 0.8 %finish.1 = (f32[3,1024]{1,0:T(4,128)}, f32[3,1024]{1,0:T(4,128)}, f32[3,1024]{1,0:T(4,128)}, f32[3,1024]{1,0:T(4,128)}, f32[8,128]{1,0:T(8,128)}, /*index=5*/f32[12,2,4096]{2,1,0:T(2,128)}) custom-call(f32[3,1024]{1,0:T(4,128)S(1)} %get-tuple-element.18.refs_0_, f32[3,1024]{1,0:T(4,128)S(1)} %get-tuple-element.19.refs_1_, ...), custom_call_target="tpu_custom_call" | custom-call | tf_op jit(solution)/shard_map/finish/pallas_call | solution.py:544

commit v5 on v4

--- a/solution.py
+++ b/solution.py
@@ -15,6 +15,7 @@
 LANES = 128
 HALF = 64
 CORES = 2
+DEPTH = 16
 RINGS = {"z": 8, "y": 8, "x": 4}
 
 
@@ -62,24 +63,21 @@
     return jnp.where(low_lanes(), low, swap(high))
 
 
-def pair_terms(act, field, sums):
+def pair_weights(act, field):
     ax, ay, az, au, av, aw = act
-    fx, fy, fz, fu, fv, fw, mass = field
+    fx, fy, fz, fu, fv, fw = field
     dx, dy, dz = fx - ax, fy - ay, fz - az
     du, dv, dw = fu - au, fv - av, fw - aw
     dist_sq = (dx * dx + dy * dy) + (dz * dz + SOFT_SQ)
     inv = lax.rsqrt(dist_sq)
     inv_sq = inv * inv
-    weight = (mass * inv) * inv_sq
-    radial = ((dx * du + dy * dv) + dz * dw) * (3.0 * inv_sq)
-    return (
-        sums[0] + weight * dx,
-        sums[1] + weight * dy,
-        sums[2] + weight * dz,
-        sums[3] + weight * (du - radial * dx),
-        sums[4] + weight * (dv - radial * dy),
-        sums[5] + weight * (dw - radial * dz),
-    )
+    cubed = inv * inv_sq
+    return cubed, (((dx * du + dy * dv) + dz * dw) * inv_sq) * cubed
+
+
+def split2(value):
+    first = value.astype(BF16)
+    return first, (value - first.astype(F32)).astype(BF16)
 
 
 def hops(delta, size):
@@ -92,9 +90,9 @@
     pos_out, vel_out, acc_out, jerk_out, time_out, state_out,
     pos_v, vel_v, acc_v, jerk_v, mass_v, last_v, act_v,
     raw, src0, rs_src, rs_dst, pick_src, pick_dst, sum_src, sum_dst,
-    field, gath, act_cols, sums_v, corr, low_hot, match, column, scat, fresh, left,
+    field, gath, act_cols, feat, centre, corr, low_hot, match, column, scat, fresh, left, left_c, right_c, ahead, coming,
     in_sem, rs_s, rs_r, pick_s, pick_r, sum_s, sum_r, fz_s, fz_r, fc_s, fc_r,
-    ag_s, ag_r, agc_s, agc_r,
+    ag_s, ag_r, agc_s, agc_r, an_s, an_r, anc_s, anc_r,
 ):
     zs, ys, xs = sizes
     total = xs * zs * LANES
@@ -182,6 +180,10 @@
     src0[48:56, :] = elapsed0
     src0[56:112, :] = raw[56:112, :]
     lay_field(0, rows0, value(raw, 7))
+    for n, row in enumerate(rows0):
+        middle = jnp.sum(jnp.sum(row, axis=0, keepdims=True), axis=1, keepdims=True) / (8.0 * LANES)
+        centre[n : n + 1, :] = jnp.broadcast_to(middle, (1, LANES))
+    centre[6:8, :] = jnp.zeros((2, LANES), F32)
 
     sub = lax.broadcasted_iota(jnp.int32, (LANES, LANES), 0)
     sub8 = lax.broadcasted_iota(jnp.int32, (8, LANES), 0)
@@ -267,100 +269,196 @@
         for comp in range(6):
             act_cols[comp] = jnp.broadcast_to(wide[0:HALF, comp : comp + 1], (HALF, LANES))
 
-    def forces(step, begin, end, fresh_start):
-        def group(g, _):
-            rows = pl.ds(pl.multiple_of(g * 8, 8), 8)
-            act = [act_cols[comp, rows, :] for comp in range(6)]
-
-            def tile(t, sums):
-                parts = [field[step, t, n : n + 1, :] for n in range(7)]
-                return pair_terms(act, parts, sums)
-
-            if fresh_start:
-                start = tuple(jnp.zeros((8, LANES), F32) for _ in range(6))
-            else:
-                start = tuple(sums_v[rows, n * LANES : (n + 1) * LANES] for n in range(6))
-            done = lax.fori_loop(begin, end, tile, start, unroll=16)
-            for n in range(6):
-                sums_v[rows, n * LANES : (n + 1) * LANES] = done[n]
+    def build_features(step, begin, end):
+        row = lax.broadcasted_iota(jnp.int32, (8, LANES), 0)
+
+        def one(t, _):
+            tile = field[step, t]
+            mass = tile[6:7]
+            own = jnp.where(row < 6, (tile - centre[...]) * mass, jnp.where(row == 6, mass, 0.0))
+            pieces = [piece.astype(F32) for piece in split3(own)] + [jnp.zeros((8, LANES), F32)]
+            at = pl.multiple_of(t * LANES, LANES)
+            feat[:, pl.ds(at, LANES)] = jnp.concatenate(pieces, axis=0).astype(BF16)
             return 0
 
-        lax.fori_loop(0, 8, group, 0)
-
-    def all_sums(step):
-        lane = lax.broadcasted_iota(jnp.int32, (8, 6 * LANES), 1)
-        row = lax.broadcasted_iota(jnp.int32, (8, 6 * LANES), 0)
-        ones = jnp.where(jnp.right_shift(lane, 7) == row, 1.0, 0.0).astype(BF16)
-        one, two, three = split3(sums_v[...])
-        rows = (dot_nt(ones, three) + dot_nt(ones, two)) + dot_nt(ones, one)
-        sum_src[step] = jnp.concatenate([rows, jnp.zeros((8, HALF), F32)], axis=1)
+        lax.fori_loop(begin, end, one, 0, unroll=4 if (end - begin) % 4 == 0 else 2)
+
+    def forces(step, tile, tiles):
+        def weights(t):
+            parts = {key: [] for key in ("w_hi", "w_lo", "q_hi", "q_lo")}
+            for pair in range(4):
+                ws, qs = [], []
+                for k in range(2):
+                    near = [field[step, t * 2 + k, n : n + 1, :] for n in range(6)]
+                    both = [
+                        pair_weights([act_cols[n, g * 8 : g * 8 + 8, :] for n in range(6)], near)
+                        for g in (2 * pair, 2 * pair + 1)
+                    ]
+                    ws.append(jnp.concatenate([b[0] for b in both], axis=0))
+                    qs.append(jnp.concatenate([b[1] for b in both], axis=0))
+                for key, cols in (("w", ws), ("q", qs)):
+                    high, low = split2(jnp.concatenate(cols, axis=1))
+                    parts[key + "_hi"].append(high)
+                    parts[key + "_lo"].append(low)
+            return (jnp.concatenate(parts["w_hi"] + parts["q_hi"], axis=0),
+                    jnp.concatenate(parts["w_lo"] + parts["q_lo"], axis=0))
+
+        def add(sums, t, pieces):
+            here = feat[:, pl.ds(pl.multiple_of(t * 2 * LANES, 2 * LANES), 2 * LANES)]
+            return tuple(total + dot_nt(here, piece) for total, piece in zip(sums, pieces))
+
+        def run_of(first, count, sums):
+            held = None
+            for n in range(count):
+                now = weights(first + n)
+                if held is not None:
+                    sums = add(sums, first + n - 1, held)
+                held = now
+            return add(sums, first + count - 1, held)
+
+        whole, rest = divmod(tiles // 2, DEPTH)
+        sums = (jnp.zeros((32, LANES), F32), jnp.zeros((32, LANES), F32))
+        if whole:
+            sums = lax.fori_loop(0, whole, lambda n, held: run_of(n * DEPTH, DEPTH, held), sums)
+        if rest:
+            sums = run_of(whole * DEPTH, rest, sums)
+        both = sums[0] + sums[1]
+        by_w = (both[16:24] + both[8:16]) + both[0:8]
+        by_q = swap(by_w)
+        off = tile - centre[...]
+        acc = by_w[0:3] - off[0:3] * by_w[6:7]
+        jerk = (by_w[3:6] - off[3:6] * by_w[6:7]) - 3.0 * (by_q[0:3] - off[0:3] * by_q[6:7])
+        low = lax.broadcasted_iota(jnp.int32, (3, LANES), 1) < HALF
+        sum_src[step, 0:3] = jnp.where(low, acc, swap(jerk))
+
+    def send_sums(step):
         return [
-            send(sum_src.at[step], sum_dst.at[step, y], sum_s.at[step, dy], sum_r.at[step, y],
+            send(sum_src.at[step, pl.ds(0, 3)], sum_dst.at[step, y, pl.ds(0, 3)],
+                 sum_s.at[step, dy], sum_r.at[step, y],
                  device(0, dy, 0, 0))
             for dy in y_list
         ]
 
     def total_sums(step, copies):
-        sum_dst[step, y] = sum_src[step]
+        sum_dst[step, y, 0:3] = sum_src[step, 0:3]
         for dy in y_list:
             other = lax.rem(y + dy, ys)
             pltpu.make_async_remote_copy(
-                src_ref=sum_src.at[step], dst_ref=sum_dst.at[step, other],
+                src_ref=sum_src.at[step, pl.ds(0, 3)],
+                dst_ref=sum_dst.at[step, other, pl.ds(0, 3)],
                 send_sem=sum_s.at[step, dy], recv_sem=sum_r.at[step, other],
                 device_id=device(0, dy, 0, 0), device_id_type=MESH,
             ).wait_recv()
-        tile = sum_dst[step, 0]
+        tile = sum_dst[step, 0, 0:3]
         for n in range(1, ys):
-            tile = tile + sum_dst[step, n]
-        return tile
+            tile = tile + sum_dst[step, n, 0:3]
+        return tile, swap(tile)
 
     def correct(act, force):
         other = swap(act)
         pred_pos, pred_vel, mass = act[0:3], act[3:6], act[7:8]
         elapsed = jnp.where(low_lanes()[0:1], act[6:7], 1.0)
         old_acc, old_jerk = other[0:3], other[3:6]
-        new_acc, new_jerk = force[0:3], force[3:6]
+        new_acc, new_jerk = force
         sq = elapsed * elapsed
         diff = old_acc - new_acc
         snap = (-6.0 * diff - elapsed * (4.0 * old_jerk + 2.0 * new_jerk)) / sq
         crackle = (12.0 * diff + 6.0 * elapsed * (old_jerk + new_jerk)) / (sq * elapsed)
         pos = pred_pos + sq * sq / 24.0 * snap + sq * sq * elapsed / 120.0 * crackle
         vel = pred_vel + sq * elapsed / 6.0 * snap + sq * sq / 24.0 * crackle
-        one = jnp.ones((1, LANES), F32)
-        low = jnp.concatenate([pos, vel, one, mass], axis=0)
-        high = jnp.concatenate([new_acc, new_jerk, one, one], axis=0)
-        return pack(low, high)
-
-    def gather_fresh(step, tile):
-        gath[step, 0, 0, 0] = tile
-        copies = {}
-        for dz, dx in xz_list:
-            copies[dz, dx] = send(
-                gath.at[step, 0, 0, 0], gath.at[step, 0, dz, dx], ag_s.at[step, dz, dx],
-                ag_r.at[step, dz, dx], device(dz, 0, 0, dx),
+        return pos, vel, new_acc, new_jerk
+
+    def gather_fresh(step, rows):
+        two = jnp.ones((2, LANES), F32)
+        gath[step, 0, 0, 0] = pack(
+            jnp.concatenate([rows[0], rows[1], two], axis=0),
+            jnp.concatenate([rows[2], rows[3], two], axis=0),
+        )
+        return {
+            (dz, dx): send(
+                gath.at[step, 0, 0, 0, pl.ds(0, 6)], gath.at[step, 0, dz, dx, pl.ds(0, 6)],
+                ag_s.at[step, dz, dx], ag_r.at[step, dz, dx], device(dz, 0, 0, dx),
             )
-        return copies
-
-    def finish_gather(step, copies):
+            for dz, dx in xz_list
+        }
+
+    def gather_next(rows, mass):
+        pos, vel = predict(*rows, 2 * STEP - STEP)
+        all_rows = jnp.concatenate([pos, vel, mass, jnp.ones((1, LANES), F32)], axis=0)
+        low = lax.broadcasted_iota(jnp.int32, (4, LANES), 1) < HALF
+        ahead[0, 0, 0] = jnp.where(low, all_rows[0:4], swap(all_rows)[4:8])
+        return {
+            (dz, dx): send(
+                ahead.at[0, 0, 0], ahead.at[0, dz, dx],
+                an_s.at[dz, dx], an_r.at[dz, dx], device(dz, 0, 0, dx),
+            )
+            for dz, dx in xz_list
+        }
+
+    def by_chunks(copies, forward_chunk, take):
+        order = [0] + z_list
         across = []
-        for dz in [0] + z_list:
+        for n, dz in enumerate(order):
             for dx in range(xs):
                 if (dz, dx) != (0, 0):
                     copies[dz, dx].wait_recv()
-            across.append(
-                send(gath.at[step, 0, dz], gath.at[step, 1, dz], agc_s.at[step, dz],
-                     agc_r.at[step, dz], device(0, 0, 1, 0))
-            )
-        for copy in across:
+            across.append(forward_chunk(dz))
+        for copy, dz in zip(across, order):
             copy.wait_recv()
-        for px in range(xs):
-            for pz in range(zs):
-                dz, dx = lax.rem(z - pz + zs, zs), lax.rem(x - px + xs, xs)
-                tile0 = gath[step, c, dz, dx]
-                tile1 = gath[step, 1 - c, dz, dx]
-                at = (px * zs + pz) * LANES
-                corr[step, 0:8, at : at + LANES] = jnp.where(low_lanes(), tile0, swap(tile1))
-                corr[step, 8:16, at : at + LANES] = jnp.where(low_lanes(), swap(tile0), tile1)
+            take(dz)
+
+    def forward_fresh(step):
+        return lambda dz: send(
+            gath.at[step, 0, dz, :, pl.ds(0, 6)], gath.at[step, 1, dz, :, pl.ds(0, 6)],
+            agc_s.at[step, dz], agc_r.at[step, dz], device(0, 0, 1, 0),
+        )
+
+    def forward_next(dz):
+        return send(ahead.at[0, dz], ahead.at[1, dz], anc_s.at[dz], anc_r.at[dz], device(0, 0, 1, 0))
+
+    def place_of(dz, dx):
+        pz, px = lax.rem(z - dz + zs, zs), lax.rem(x - dx + xs, xs)
+        return pl.multiple_of((px * zs + pz) * LANES, LANES)
+
+    def take_next(dz):
+        low = lax.broadcasted_iota(jnp.int32, (4, LANES), 1) < HALF
+        for dx in range(xs):
+            at = place_of(dz, dx)
+            tile0, tile1 = ahead[c, dz, dx], ahead[1 - c, dz, dx]
+            coming[0:4, pl.ds(at, LANES)] = jnp.where(low, tile0, swap(tile1))
+            coming[4:8, pl.ds(at, LANES)] = jnp.where(low, swap(tile0), tile1)
+
+    def both_cores(step, dz, dx):
+        tile0, tile1 = gath[step, c, dz, dx], gath[step, 1 - c, dz, dx]
+        return (jnp.where(low_lanes(), tile0, swap(tile1)),
+                jnp.where(low_lanes(), swap(tile0), tile1))
+
+    def take_fresh(dz):
+        for dx in range(xs):
+            at = place_of(dz, dx)
+            low, high = both_cores(0, dz, dx)
+            corr[0:8, pl.ds(at, LANES)] = low
+            corr[8:16, pl.ds(at, LANES)] = high
+
+    def masked_pieces(step, at, low, high):
+        mine = high_hot(step, at)
+        rows = []
+        for piece in split3(jnp.concatenate([low, high], axis=0)):
+            wide = piece.astype(F32)
+            rows += [jnp.where(mine, wide[v : v + 1], 0.0) for v in names]
+        return jnp.concatenate(rows, axis=0).astype(BF16)
+
+    def take_last(dz):
+        for dx in range(xs):
+            at = place_of(dz, dx)
+            low, high = both_cores(1, dz, dx)
+            for n in range(6):
+                state_out[n, 1:2, pl.ds(at, LANES)] = low[n : n + 1]
+                state_out[6 + n, 1:2, pl.ds(at, LANES)] = high[n : n + 1]
+            here = slice(dx * LANES, (dx + 1) * LANES)
+            left_c[:, here] = masked_pieces(1, at, low, high)
+            right_c[:, here] = low_hot[1, :, pl.ds(at, LANES)]
+        scat[...] += dot_nt(left_c[...], right_c[...])
 
     chunks = total // LANES
     names = [0, 1, 2, 3, 4, 5, 8, 9, 10, 11, 12, 13]
@@ -397,29 +495,26 @@
 
         lax.fori_loop(0, chunks, one, 0)
 
-    def place(step, hit):
+    def settle(step):
+        taken = fresh[step] > 0.5
+        for n, v in enumerate(names):
+            at, row = v * 8, n * 8
+            new = (scat[192 + row : 200 + row, :] + scat[96 + row : 104 + row, :]) + scat[row : row + 8, :]
+            raw[at : at + 8, :] = jnp.where(taken, new, raw[at : at + 8, :])
+        raw[48:56, :] = jnp.where(taken, STEP * (step + 1), raw[48:56, :])
+
+    def place_first():
         def one(n, _):
             at = pl.multiple_of(n * LANES, LANES)
-            mine = high_hot(step, at)
-            pieces = split3(corr[step, :, pl.ds(at, LANES)])
-            for p, piece in enumerate(pieces):
-                wide = piece.astype(F32)
-                rows = [jnp.where(mine, wide[v : v + 1], 0.0) for v in names]
-                left[p * 96 : p * 96 + 96, pl.ds(at, LANES)] = jnp.concatenate(rows, axis=0).astype(BF16)
+            tiles = corr[:, pl.ds(at, LANES)]
+            left[:, pl.ds(at, LANES)] = masked_pieces(0, at, tiles[0:8], tiles[8:16])
             return 0
 
         lax.fori_loop(0, chunks, one, 0, unroll=2)
-        got = dot_nt(left[...], low_hot[step])
-        scat[...] = (got[192:288] + got[96:192]) + got[0:96]
-        taken = hit > 0.5
+        scat[...] = dot_nt(left[...], low_hot[0])
+        settle(0)
         for n, v in enumerate(names):
-            at = v * 8
-            raw[at : at + 8, :] = jnp.where(taken, scat[n * 8 : n * 8 + 8, :], raw[at : at + 8, :])
-        raw[48:56, :] = jnp.where(taken, STEP * (step + 1), raw[48:56, :])
-
-    def write_state(step):
-        for n, v in enumerate(names):
-            state_out[n, step : step + 1, :] = corr[step, v : v + 1, :]
+            state_out[n, 0:1, :] = corr[v : v + 1, :]
 
     pick(0, src0)
     pl.semaphore_wait(barrier, len(partners))
@@ -433,55 +528,59 @@
     rows1, _ = predicted(2 * STEP)
     lay_field(1, rows1, jnp.where(hit0 > 0.5, 0.0, value(raw, 7)))
     pass_on(0, f0, across0)
+    build_features(0, 0, zs * block)
     act0 = picked(0, ar0)
     rs1 = scatter_picks(1)
     f1, across1 = send_field(1)
     set_columns(act0)
-    forces(0, 0, zs * block, True)
     for copy in across0:
         copy.wait_recv()
-    forces(0, zs * block, 2 * zs * block, False)
-    s0 = all_sums(0)
+    build_features(0, zs * block, 2 * zs * block)
+    forces(0, act0, 2 * zs * block)
+    s0 = send_sums(0)
     ar1 = reduce_picks(1, rs1)
     build_match()
     force0 = total_sums(0, s0)
-    fresh0 = gather_fresh(0, correct(act0, force0))
+    rows_a = correct(act0, force0)
+    next0 = gather_next(rows_a, act0[7:8])
+    fresh0 = gather_fresh(0, rows_a)
     pass_on(1, f1, across1)
     build_low_hot(1)
     fresh[1] = hits(1)
     act1_raw = picked(1, ar1)
+    raw_high = swap(act1_raw)
+    raw_elapsed = 2 * STEP - act1_raw[6:7]
+    raw_pos, raw_vel = predict(
+        act1_raw[0:3], act1_raw[3:6], raw_high[0:3], raw_high[3:6], raw_elapsed
+    )
     for copy in across1:
         copy.wait_recv()
-    finish_gather(0, fresh0)
+    build_features(1, 0, 2 * zs * block)
+    by_chunks(next0, forward_next, take_next)
 
     extra = total // ys
     for n in range(extra // LANES):
         at = pl.multiple_of(y * extra + n * LANES, LANES)
-        low = corr[0, 0:8, pl.ds(at, LANES)]
-        high = corr[0, 8:16, pl.ds(at, LANES)]
-        new_pos, new_vel = predict(low[0:3], low[3:6], high[0:3], high[3:6], 2 * STEP - STEP)
-        field[1, 2 * zs * block + n] = jnp.concatenate(
-            [new_pos, new_vel, low[7:8], jnp.zeros((1, LANES), F32)], axis=0
-        )
-    found = exact_nt(corr[0], match[...])
-    found = jnp.concatenate([found, jnp.zeros((16, HALF), F32)], axis=1)
-    again = found[14:15] > 0.5
-    low = jnp.where(again, found[0:8], act1_raw)
-    high = jnp.where(again, found[8:16], swap(act1_raw))
-    last = jnp.where(again, STEP, act1_raw[6:7])
-    elapsed1 = 2 * STEP - last
-    pos1, vel1 = predict(low[0:3], low[3:6], high[0:3], high[3:6], elapsed1)
-    act1 = pack(jnp.concatenate([pos1, vel1, elapsed1, low[7:8]], axis=0), high)
-    set_columns(act1)
-    forces(1, 0, 2 * zs * block + extra // LANES, True)
-    s1 = all_sums(1)
-    place(0, fresh[0])
-    write_state(0)
+        field[1, 2 * zs * block + n] = coming[:, pl.ds(at, LANES)]
+    found = exact_nt(coming[...], match[...])
+    found = jnp.concatenate([found, jnp.zeros((8, HALF), F32)], axis=1)
+    again = found[7:8] > 0.5
+    elapsed1 = jnp.where(again, 2 * STEP - STEP, raw_elapsed)
+    ahead1 = jnp.where(again, found[0:6], jnp.concatenate([raw_pos, raw_vel], axis=0))
+    low1 = jnp.concatenate([ahead1, elapsed1, act1_raw[7:8]], axis=0)
+    set_columns(low1)
+    build_features(1, 2 * zs * block, 2 * zs * block + extra // LANES)
+    forces(1, low1, 2 * zs * block + extra // LANES)
+    s1 = send_sums(1)
+    by_chunks(fresh0, forward_fresh(0), take_fresh)
+    held = jnp.concatenate([exact_nt(corr[8:16, :], match[...]), jnp.zeros((8, HALF), F32)], axis=1)
+    act1 = pack(low1, jnp.where(again, held, raw_high))
     force1 = total_sums(1, s1)
     fresh1 = gather_fresh(1, correct(act1, force1))
-    finish_gather(1, fresh1)
-    write_state(1)
-    place(1, fresh[1])
+    place_first()
+    scat[...] = jnp.zeros((288, LANES), F32)
+    by_chunks(fresh1, forward_fresh(1), take_last)
+    settle(1)
     for ref, at in ((pos_out, 0), (vel_out, 3), (acc_out, 8), (jerk_out, 11)):
         for comp in range(3):
             for hi in range(8):
@@ -516,15 +615,17 @@
         vmem((2, 8, LANES), F32), vmem((2, ys, 8, LANES), F32),
         vmem((2, tiles, 8, LANES), F32),
         vmem((2, CORES, zs, xs, 8, LANES), F32),
-        vmem((6, HALF, LANES), F32), vmem((HALF, 6 * LANES), F32),
-        vmem((2, 16, total), F32), vmem((2, LANES, total), BF16), vmem((HALF, total), BF16),
-        vmem((LANES, LANES), F32), vmem((96, LANES), F32), vmem((2, 8, LANES), F32),
-        vmem((288, total), BF16),
+        vmem((6, HALF, LANES), F32), vmem((32, tiles * LANES), BF16), vmem((8, LANES), F32),
+        vmem((16, total), F32), vmem((2, LANES, total), BF16), vmem((HALF, total), BF16),
+        vmem((LANES, LANES), F32), vmem((288, LANES), F32), vmem((2, 8, LANES), F32),
+        vmem((288, total), BF16), vmem((288, xs * LANES), BF16), vmem((LANES, xs * LANES), BF16),
+        vmem((CORES, zs, xs, 4, LANES), F32), vmem((8, total), F32),
         dma((7,)),
         dma((2, zs, CORES)), dma((2, zs, CORES)),
         dma((2, ys)), dma((2, ys)), dma((2, ys)), dma((2, ys)),
         dma((2, zs)), dma((2, zs)), dma((2, zs)), dma((2, zs)),
         dma((2, zs, xs)), dma((2, zs, xs)), dma((2, zs)), dma((2, zs)),
+        dma((zs, xs)), dma((zs, xs)), dma((zs,)), dma((zs,)),
     ]
     flat = jax.ShapeDtypeStruct((3, 1024), F32)
     out_shape = [flat, flat, flat, flat, jax.ShapeDtypeStruct((8, LANES), F32),

time: 71.6 us -> 68.1 us (0.951)
  Pallas kernels: 70.8 us -> 67.3 us
    pallas_call x1, Pallas kernels: 70 us -> 66.5 us  [run(): pl.pallas_call(functools.partial(kernel, sizes), out_shape=[pltpu.VMEM(ou...]
where the time goes in v5:
time: 68.1 us; the launch traced here: 67.9 us
  Pallas kernels  67.3 us (99%)
    pallas_call x1, Pallas kernels, run(): pl.pallas_call(functools.partial(kernel, sizes), out_shape=[pltpu.VMEM(ou...  66.5 us

profile of v5, /device:TPU:1, one launch (start us, length us, event | category | flops | bytes accessed | tf_op | source)
XLA Modules:
  0.0 67.9 jit_solution(14227389958330147434)
XLA Ops:
  0.6 66.5 %hermite.1 = (f32[3,1024]{1,0:T(4,128)S(1)}, f32[3,1024]{1,0:T(4,128)S(1)}, f32[3,1024]{1,0:T(4,128)S(1)}, f32[3,1024]{1,0:T(4,128)S(1)}, f32[8,128]{1,0:T(8,128)S(1)}, /*index=5*/f32[12,2,4096]{2,1,0:T(2,128)S(1)}) custom-call(f32[3,1024]{1,0:T(4,128)} %pos_in.1, f32[3,1024]{1,0:T(4,128)} %vel_in.1, f32[3,1024]{1,0:T(4,128)} %acc_in.1, f32[3,1024]{1,0:T(4,128)} %jerk_in.1, ...), custom_call_target="tpu_custom_call" | custom-call | tf_op jit(solution)/shard_map/hermite/pallas_call | solution.py:634
  67.1 0.8 %finish.1 = (f32[3,1024]{1,0:T(4,128)}, f32[3,1024]{1,0:T(4,128)}, f32[3,1024]{1,0:T(4,128)}, f32[3,1024]{1,0:T(4,128)}, f32[8,128]{1,0:T(8,128)}, /*index=5*/f32[12,2,4096]{2,1,0:T(2,128)}) custom-call(f32[3,1024]{1,0:T(4,128)S(1)} %get-tuple-element.18.refs_0_, f32[3,1024]{1,0:T(4,128)S(1)} %get-tuple-element.19.refs_1_, ...), custom_call_target="tpu_custom_call" | custom-call | tf_op jit(solution)/shard_map/finish/pallas_call | solution.py:645

commit v6 on v5

--- a/solution.py
+++ b/solution.py
@@ -15,7 +15,7 @@
 LANES = 128
 HALF = 64
 CORES = 2
-DEPTH = 16
+DEPTH = 32
 RINGS = {"z": 8, "y": 8, "x": 4}
 
 
@@ -92,7 +92,7 @@
     raw, src0, rs_src, rs_dst, pick_src, pick_dst, sum_src, sum_dst,
     field, gath, act_cols, feat, centre, corr, low_hot, match, column, scat, fresh, left, left_c, right_c, ahead, coming,
     in_sem, rs_s, rs_r, pick_s, pick_r, sum_s, sum_r, fz_s, fz_r, fc_s, fc_r,
-    ag_s, ag_r, agc_s, agc_r, an_s, an_r, anc_s, anc_r,
+    met, ag_s, ag_r, agc_s, agc_r, an_s, an_r, anc_s, anc_r,
 ):
     zs, ys, xs = sizes
     total = xs * zs * LANES
@@ -120,6 +120,12 @@
     y_list = sorted(range(1, ys), key=lambda p: -hops(p, ys))
     z_list = sorted(range(1, zs), key=lambda p: hops(p, zs))
     started = []
+    drained = []
+
+    def drain(count):
+        for copy in started[len(drained) : count]:
+            copy.wait_send()
+            drained.append(copy)
 
     def send(src, dst, ssem, rsem, target):
         copy = pltpu.make_async_remote_copy(
@@ -142,7 +148,7 @@
     barrier = pltpu.get_barrier_semaphore()
     partners = [(dz, 0, dc, 0) for dz, dc in zc_list]
     partners += [(0, dy, 0, 0) for dy in y_list]
-    partners += [(dz, 0, 0, dx) for dz, dx in xz_list if dx != 0]
+    partners += [(0, 0, 0, dx) for dx in range(1, xs)]
     for partner in partners:
         pl.semaphore_signal(barrier, inc=1, device_id=device(*partner), device_id_type=MESH)
     for load in loads:
@@ -179,11 +185,6 @@
         src0[n * 8 : n * 8 + 8, :] = row
     src0[48:56, :] = elapsed0
     src0[56:112, :] = raw[56:112, :]
-    lay_field(0, rows0, value(raw, 7))
-    for n, row in enumerate(rows0):
-        middle = jnp.sum(jnp.sum(row, axis=0, keepdims=True), axis=1, keepdims=True) / (8.0 * LANES)
-        centre[n : n + 1, :] = jnp.broadcast_to(middle, (1, LANES))
-    centre[6:8, :] = jnp.zeros((2, LANES), F32)
 
     sub = lax.broadcasted_iota(jnp.int32, (LANES, LANES), 0)
     sub8 = lax.broadcasted_iota(jnp.int32, (8, LANES), 0)
@@ -519,10 +520,17 @@
     pick(0, src0)
     pl.semaphore_wait(barrier, len(partners))
     rs0 = scatter_picks(0)
+    lay_field(0, rows0, value(raw, 7))
     f0, across0 = send_field(0)
+    for n, row in enumerate(rows0):
+        middle = jnp.sum(jnp.sum(row, axis=0, keepdims=True), axis=1, keepdims=True) / (8.0 * LANES)
+        centre[n : n + 1, :] = jnp.broadcast_to(middle, (1, LANES))
+    centre[6:8, :] = jnp.zeros((2, LANES), F32)
     pick(1, raw)
     build_low_hot(0)
     ar0 = reduce_picks(0, rs0)
+    for dx in range(1, xs):
+        pl.semaphore_signal(met, inc=1, device_id=device(0, 0, 0, dx), device_id_type=MESH)
     hit0 = hits(0)
     fresh[0] = hit0
     rows1, _ = predicted(2 * STEP)
@@ -537,16 +545,19 @@
         copy.wait_recv()
     build_features(0, zs * block, 2 * zs * block)
     forces(0, act0, 2 * zs * block)
+    early = len(started)
     s0 = send_sums(0)
     ar1 = reduce_picks(1, rs1)
     build_match()
     force0 = total_sums(0, s0)
     rows_a = correct(act0, force0)
+    pl.semaphore_wait(met, xs - 1)
     next0 = gather_next(rows_a, act0[7:8])
     fresh0 = gather_fresh(0, rows_a)
     pass_on(1, f1, across1)
     build_low_hot(1)
     fresh[1] = hits(1)
+    drain(early)
     act1_raw = picked(1, ar1)
     raw_high = swap(act1_raw)
     raw_elapsed = 2 * STEP - act1_raw[6:7]
@@ -576,8 +587,10 @@
     held = jnp.concatenate([exact_nt(corr[8:16, :], match[...]), jnp.zeros((8, HALF), F32)], axis=1)
     act1 = pack(low1, jnp.where(again, held, raw_high))
     force1 = total_sums(1, s1)
+    late = len(started)
     fresh1 = gather_fresh(1, correct(act1, force1))
     place_first()
+    drain(late)
     scat[...] = jnp.zeros((288, LANES), F32)
     by_chunks(fresh1, forward_fresh(1), take_last)
     settle(1)
@@ -587,8 +600,7 @@
                 row = (at + comp) * 8 + hi
                 ref[comp : comp + 1, hi * LANES : (hi + 1) * LANES] = raw[row : row + 1, :]
     time_out[...] = raw[48:56, :]
-    for copy in started:
-        copy.wait_send()
+    drain(len(started))
 
 
 def hand_on(*refs):
@@ -624,6 +636,7 @@
         dma((2, zs, CORES)), dma((2, zs, CORES)),
         dma((2, ys)), dma((2, ys)), dma((2, ys)), dma((2, ys)),
         dma((2, zs)), dma((2, zs)), dma((2, zs)), dma((2, zs)),
+        pltpu.SemaphoreType.REGULAR,
         dma((2, zs, xs)), dma((2, zs, xs)), dma((2, zs)), dma((2, zs)),
         dma((zs, xs)), dma((zs, xs)), dma((zs,)), dma((zs,)),
     ]

time: 68.1 us -> 67.2 us (0.987)
  Pallas kernels: 67.3 us -> 66.4 us
    pallas_call x1, Pallas kernels: 66.5 us -> 65.5 us  [run(): pl.pallas_call(functools.partial(kernel, sizes), out_shape=[pltpu.VMEM(ou...]
where the time goes in v6:
time: 67.2 us; the launch traced here: 67 us
  Pallas kernels  66.4 us (99%)
    pallas_call x1, Pallas kernels, run(): pl.pallas_call(functools.partial(kernel, sizes), out_shape=[pltpu.VMEM(ou...  65.5 us

profile of v6, /device:TPU:1, one launch (start us, length us, event | category | flops | bytes accessed | tf_op | source)
XLA Modules:
  0.0 67.0 jit_solution(2812642256186596873)
XLA Ops:
  0.6 65.5 %hermite.1 = (f32[3,1024]{1,0:T(4,128)S(1)}, f32[3,1024]{1,0:T(4,128)S(1)}, f32[3,1024]{1,0:T(4,128)S(1)}, f32[3,1024]{1,0:T(4,128)S(1)}, f32[8,128]{1,0:T(8,128)S(1)}, /*index=5*/f32[12,2,4096]{2,1,0:T(2,128)S(1)}) custom-call(f32[3,1024]{1,0:T(4,128)} %pos_in.1, f32[3,1024]{1,0:T(4,128)} %vel_in.1, f32[3,1024]{1,0:T(4,128)} %acc_in.1, f32[3,1024]{1,0:T(4,128)} %jerk_in.1, ...), custom_call_target="tpu_custom_call" | custom-call | tf_op jit(solution)/shard_map/hermite/pallas_call | solution.py:647
  66.2 0.8 %finish.1 = (f32[3,1024]{1,0:T(4,128)}, f32[3,1024]{1,0:T(4,128)}, f32[3,1024]{1,0:T(4,128)}, f32[3,1024]{1,0:T(4,128)}, f32[8,128]{1,0:T(8,128)}, /*index=5*/f32[12,2,4096]{2,1,0:T(2,128)}) custom-call(f32[3,1024]{1,0:T(4,128)S(1)} %get-tuple-element.18.refs_0_, f32[3,1024]{1,0:T(4,128)S(1)} %get-tuple-element.19.refs_1_, ...), custom_call_target="tpu_custom_call" | custom-call | tf_op jit(solution)/shard_map/finish/pallas_call | solution.py:658

commit v7 on v6

--- a/solution.py
+++ b/solution.py
@@ -90,7 +90,7 @@
     pos_out, vel_out, acc_out, jerk_out, time_out, state_out,
     pos_v, vel_v, acc_v, jerk_v, mass_v, last_v, act_v,
     raw, src0, rs_src, rs_dst, pick_src, pick_dst, sum_src, sum_dst,
-    field, gath, act_cols, feat, centre, corr, low_hot, match, column, scat, fresh, left, left_c, right_c, ahead, coming,
+    field, gath, act_cols, feat, centre, corr, low_hot, match, column, scat, fresh, left, ahead, coming,
     in_sem, rs_s, rs_r, pick_s, pick_r, sum_s, sum_r, fz_s, fz_r, fc_s, fc_r,
     met, ag_s, ag_r, agc_s, agc_r, an_s, an_r, anc_s, anc_r,
 ):
@@ -456,10 +456,7 @@
             for n in range(6):
                 state_out[n, 1:2, pl.ds(at, LANES)] = low[n : n + 1]
                 state_out[6 + n, 1:2, pl.ds(at, LANES)] = high[n : n + 1]
-            here = slice(dx * LANES, (dx + 1) * LANES)
-            left_c[:, here] = masked_pieces(1, at, low, high)
-            right_c[:, here] = low_hot[1, :, pl.ds(at, LANES)]
-        scat[...] += dot_nt(left_c[...], right_c[...])
+            left[:, pl.ds(at, LANES)] = masked_pieces(1, at, low, high)
 
     chunks = total // LANES
     names = [0, 1, 2, 3, 4, 5, 8, 9, 10, 11, 12, 13]
@@ -591,8 +588,8 @@
     fresh1 = gather_fresh(1, correct(act1, force1))
     place_first()
     drain(late)
-    scat[...] = jnp.zeros((288, LANES), F32)
     by_chunks(fresh1, forward_fresh(1), take_last)
+    scat[...] = dot_nt(left[...], low_hot[1])
     settle(1)
     for ref, at in ((pos_out, 0), (vel_out, 3), (acc_out, 8), (jerk_out, 11)):
         for comp in range(3):
@@ -630,7 +627,7 @@
         vmem((6, HALF, LANES), F32), vmem((32, tiles * LANES), BF16), vmem((8, LANES), F32),
         vmem((16, total), F32), vmem((2, LANES, total), BF16), vmem((HALF, total), BF16),
         vmem((LANES, LANES), F32), vmem((288, LANES), F32), vmem((2, 8, LANES), F32),
-        vmem((288, total), BF16), vmem((288, xs * LANES), BF16), vmem((LANES, xs * LANES), BF16),
+        vmem((288, total), BF16),
         vmem((CORES, zs, xs, 4, LANES), F32), vmem((8, total), F32),
         dma((7,)),
         dma((2, zs, CORES)), dma((2, zs, CORES)),

time: 67.2 us -> 67.7 us (level)
  no operation moved by 1% of the time
where the time goes in v7:
time: 67.7 us; the launch traced here: 67.5 us
  Pallas kernels  66.8 us (99%)
    pallas_call x1, Pallas kernels, run(): pl.pallas_call(functools.partial(kernel, sizes), out_shape=[pltpu.VMEM(ou...  66 us

profile of v7, /device:TPU:1, one launch (start us, length us, event | category | flops | bytes accessed | tf_op | source)
XLA Modules:
  0.0 67.5 jit_solution(13008387270098012761)
XLA Ops:
  0.6 66.0 %hermite.1 = (f32[3,1024]{1,0:T(4,128)S(1)}, f32[3,1024]{1,0:T(4,128)S(1)}, f32[3,1024]{1,0:T(4,128)S(1)}, f32[3,1024]{1,0:T(4,128)S(1)}, f32[8,128]{1,0:T(8,128)S(1)}, /*index=5*/f32[12,2,4096]{2,1,0:T(2,128)S(1)}) custom-call(f32[3,1024]{1,0:T(4,128)} %pos_in.1, f32[3,1024]{1,0:T(4,128)} %vel_in.1, f32[3,1024]{1,0:T(4,128)} %acc_in.1, f32[3,1024]{1,0:T(4,128)} %jerk_in.1, ...), custom_call_target="tpu_custom_call" | custom-call | tf_op jit(solution)/shard_map/hermite/pallas_call | solution.py:644
  66.7 0.8 %finish.1 = (f32[3,1024]{1,0:T(4,128)}, f32[3,1024]{1,0:T(4,128)}, f32[3,1024]{1,0:T(4,128)}, f32[3,1024]{1,0:T(4,128)}, f32[8,128]{1,0:T(8,128)}, /*index=5*/f32[12,2,4096]{2,1,0:T(2,128)}) custom-call(f32[3,1024]{1,0:T(4,128)S(1)} %get-tuple-element.18.refs_0_, f32[3,1024]{1,0:T(4,128)S(1)} %get-tuple-element.19.refs_1_, ...), custom_call_target="tpu_custom_call" | custom-call | tf_op jit(solution)/shard_map/finish/pallas_call | solution.py:655
